TPU v7x, 32 devices: a whole 2x2x4 slice. The times are simulated.
32 devices in a mesh: grp: 4 (over z), dev: 8 (over y, x, core).
Axes of the slice: x: 2, y: 2, z: 4, core: 2. Of those that a mesh axis runs over, the one named last changes fastest.
Arguments:
- stiff_rows: bfloat16 [32, 6, 384, 384], P(('grp', 'dev')), may hold values from -0.75 to 0.75
- stiff_iface: bfloat16 [32, 2, 384, 384], P(('grp', 'dev')), may hold values from -0.75 to 0.75
- columns: int32 [32, 6], P(('grp', 'dev')), may hold values from 0 to 7, as said below
- live_count: int32 [32], P(('grp', 'dev')), may hold values from 2 to 6
- aggregate: int32 [32], P(('grp', 'dev')), may hold values from 0 to 1
- prolong: bfloat16 [32, 384, 384], P(('grp', 'dev')), may hold values from -0.3125 to 0.3125
Outputs:
- coarse_band: float32 [3072, 2304], P(('grp', 'dev'))
Inputs may be any that keep to these rules, and one draw needn't show every extreme that they name: The 6 columns of a row are distinct, the first is the row's own position p, and each lies within 3 positions of p around the cycle of 8 positions of the slab.
All inputs are finite; a program needn't handle non-finite values.
Results may differ from a plain program's by a relative error of at most 0.018.
Values may be sent and summed in bfloat16 or wider, within the bound.
No kernel may reach another device: no remote copies, remote signals or barrier semaphores. Data moves between devices by JAX's collectives and lax.ppermute only.
A program may use at most 64 MiB of HBM per device.

v0:
```python
import jax
import jax.numpy as jnp
from jax import lax
from jax.sharding import PartitionSpec as P

NB = 384
SLOTS = 6
REACH = 3
COARSE = 2


def passed_along(block, axis, distance):
    devices = range(lax.axis_size(axis))
    route = [((i - distance) % len(devices), i) for i in devices]
    return lax.ppermute(block, axis, route)


def extended(array, sides, width):
    for axis, dim in sides:
        count, length = (lax.axis_size(axis), array.shape[dim])
        up = [(i, (i + 1) % count) for i in range(count - 1)]
        down = [(j, i) for i, j in up]
        last = lax.slice_in_dim(array, length - width, length, axis=dim)
        initial = lax.slice_in_dim(array, 0, width, axis=dim)
        before = lax.ppermute(last, axis, up)
        after = lax.ppermute(initial, axis, down)
        array = jnp.concatenate([before, array, after], axis=dim)
    return array


def on_device(stiff_rows, stiff_iface, columns, live_count, aggregate, prolong):
    dev_count = lax.axis_size("dev")
    grp_count = lax.axis_size("grp")
    group_at = lax.axis_index("grp")
    place_at = lax.axis_index("dev")
    my_columns = columns[0]
    block_list = []
    agg_list = []
    for offset in range(-REACH, REACH + 1):
        if offset == 0:
            block_list.append(prolong)
            agg_list.append(aggregate)
        else:
            got = passed_along((prolong, aggregate), "dev", -offset)
            block_list.append(got[0])
            agg_list.append(got[1])
    window_blocks = jnp.concatenate(block_list, axis=0)
    window_aggs = jnp.concatenate(agg_list, axis=0)
    offsets = (my_columns - place_at + dev_count + REACH) % dev_count
    panels = jnp.take(window_blocks, offsets, axis=0)
    column_aggs = jnp.take(window_aggs, offsets, axis=0)
    slab_blocks, slab_aggs = (
        extended(prolong, (("grp", 0),), 1),
        extended(aggregate, (("grp", 0),), 1),
    )
    blocks = jnp.concatenate([panels, slab_blocks[0:1], slab_blocks[2:3]], axis=0)
    stiff = jnp.concatenate([stiff_rows[0], stiff_iface[0]], axis=0)
    qmat = jnp.einsum("kfg,kgm->kfm", stiff, blocks, preferred_element_type=jnp.float32).astype(
        jnp.bfloat16
    )
    contrib = jnp.einsum("fc,kfm->kcm", prolong[0], qmat, preferred_element_type=jnp.float32)
    low_agg = slab_aggs[0]
    up_agg = slab_aggs[2]
    targets = jnp.concatenate([column_aggs, low_agg[None], up_agg[None]])
    weights = jnp.concatenate(
        [
            (jnp.arange(SLOTS, dtype=jnp.int32) < live_count[0]).astype(jnp.float32),
            (group_at > 0).astype(jnp.float32)[None],
            (group_at < grp_count - 1).astype(jnp.float32)[None],
        ]
    )
    sides = jnp.concatenate([jnp.ones((SLOTS,), jnp.int32), jnp.array([0, 2], jnp.int32)])
    side_hot = (sides[:, None] == jnp.arange(3, dtype=jnp.int32)[None, :]).astype(jnp.float32)
    block_hot = (targets[:, None] == jnp.arange(COARSE, dtype=jnp.int32)[None, :]).astype(
        jnp.float32
    )
    placing = side_hot[:, :, None] * block_hot[:, None, :] * weights[:, None, None]
    partial_value = jnp.einsum("ksb,kcm->csbm", placing, contrib).reshape(NB, 3 * COARSE * NB)
    partial_value = partial_value.astype(jnp.bfloat16).astype(jnp.float32)
    own_hot = (jnp.arange(COARSE, dtype=jnp.int32) == aggregate[0]).astype(jnp.float32)
    spread = (own_hot[:, None, None] * partial_value[None]).reshape(COARSE * NB, 3 * COARSE * NB)
    return lax.psum_scatter(
        spread.astype(jnp.bfloat16), "dev", scatter_dimension=0, tiled=True
    ).astype(jnp.float32)


def solution(mesh):
    in_specs = (
        P(("grp", "dev"), None, None, None),
        P(("grp", "dev"), None, None, None),
        P(("grp", "dev"), None),
        P(("grp", "dev")),
        P(("grp", "dev")),
        P(("grp", "dev"), None, None),
    )
    out_specs = P(("grp", "dev"), None)
    return jax.shard_map(
        on_device, mesh=mesh, in_specs=in_specs, out_specs=out_specs, check_vma=False
    )
```

profile of v0, /device:TPU:0, one launch (start us, length us, event | category | flops | bytes accessed | tf_op | source)
XLA Modules:
  0.0 135.8 jit_solution(9769250324126156769)
XLA Ops:
  7.0 2.9 %collective-permute-start.11 = (s32[1]{0:T(128)}, s32[1]{0:T(128)}, u32[]{:S(2)}, u32[]{:S(2)}) collective-permute-start(s32[1]{0:T(128)} %param.11), channel_id=1, source_target_pairs={{1,0},{2,1},{3,2},{4,3},{5,4},{6,5},{7,6},{0,7},{9,8},{10,9},{11,1... | collective-permute-start | bytes 20 | tf_op jit(solution)/shard_map/ppermute | solution.py:15
  9.9 2.3 %collective-permute-start.12 = (s32[1]{0:T(128)}, s32[1]{0:T(128)}, u32[]{:S(2)}, u32[]{:S(2)}) collective-permute-start(s32[1]{0:T(128)} %param.11), channel_id=1, source_target_pairs={{2,0},{3,1},{4,2},{5,3},{6,4},{7,5},{0,6},{1,7},{10,8},{11,9},{12,... | collective-permute-start | bytes 20 | tf_op jit(solution)/shard_map/ppermute | solution.py:15
  12.2 1.7 %collective-permute-start.8 = (s32[1]{0:T(128)}, s32[1]{0:T(128)}, u32[]{:S(2)}, u32[]{:S(2)}) collective-permute-start(s32[1]{0:T(128)} %param.11), channel_id=1, source_target_pairs={{5,0},{6,1},{7,2},{0,3},{1,4},{2,5},{3,6},{4,7},{13,8},{14,9},{15,... | collective-permute-start | bytes 20 | tf_op jit(solution)/shard_map/ppermute | solution.py:15
  17.4 0.8 collective-permute-start.1
  18.3 1.3 collective-permute-start.2
  19.6 2.0 %collective-permute-start.3 = (bf16[1,384,384]{2,1,0:T(8,128)(2,1)}, bf16[1,384,384]{2,1,0:T(8,128)(2,1)S(1)}, u32[]{:S(2)}, u32[]{:S(2)}) collective-permute-start(bf16[1,384,384]{2,1,0:T(8,128)(2,1)} %param.12), channel_id=1, source_target_pairs={{1,0},{2,1},{3,2},{4,3},{5,4},{6,5},{7,6},{0,7},{9,8},{10,9},{11,1... | collective-permute-start | bytes 884744 | tf_op jit(solution)/shard_map/ppermute | solution.py:15
  21.6 4.0 %collective-permute-start.14 = (s32[1]{0:T(128)}, s32[1]{0:T(128)}, u32[]{:S(2)}, u32[]{:S(2)}) collective-permute-start(s32[1]{0:T(128)} %param.11), channel_id=1, source_target_pairs={{0,8},{8,16},{16,24},{1,9},{9,17},{17,25},{2,10},{10,18},{18,26},{... | collective-permute-start | bytes 20 | tf_op jit(solution)/shard_map/ppermute | solution.py:25
  25.6 3.9 %concatenate.28 = s32[7]{0:T(128)S(1)} concatenate(s32[1]{0:T(128)} %collective-permute-done.8, s32[1]{0:T(128)} %collective-permute-done.9, s32[1]{0:T(128)} %collective-permute-done.10, s32[1]{0:T(128)} %copy.19, s32[1]{0:T(128)} %collective-permute-done.11, s32[1]{0:T(128)} %collective-permute-done.12, s32[1]{0:T(128)} %collective-permute-done.13), dimensions={0} | concatenate | bytes 56 | tf_op jit(solution)/shard_map/concatenate | solution.py:48
  30.8 1.3 collective-permute-start.15
  32.1 4.2 %collective-permute-done.15 = s32[1]{0:T(128)} collective-permute-done((s32[1]{0:T(128)}, s32[1]{0:T(128)}, u32[]{:S(2)}, u32[]{:S(2)}) %collective-permute-start.15) | collective-permute-done | bytes 36 | tf_op jit(solution)/shard_map/ppermute | solution.py:26
  36.3 0.8 collective-permute-start.4
  37.1 1.4 %pad_add_fusion = s32[8]{0:T(128)S(1)} fusion(s32[1]{0:T(128)} %collective-permute-done.15, s32[1]{0:T(128)} %collective-permute-done.14, s32[6]{0:T(128)S(1)} %get-tuple-element.5), kind=kLoop, calls=%fused_computation.51 | loop fusion | flops 16 | bytes 64 | tf_op jit(solution)/shard_map/concatenate | solution.py:64
  39.8 3.7 %collective-permute-start.6 = (bf16[1,384,384]{2,1,0:T(8,128)(2,1)}, bf16[1,384,384]{2,1,0:T(8,128)(2,1)}, u32[]{:S(2)}, u32[]{:S(2)}) collective-permute-start(bf16[1,384,384]{2,1,0:T(8,128)(2,1)} %param.12), channel_id=1, source_target_pairs={{0,8},{8,16},{16,24},{1,9},{9,17},{17,25},{2,10},{10,18},{18,26},{... | collective-permute-start | bytes 884744 | tf_op jit(solution)/shard_map/ppermute | solution.py:25
  44.2 1.3 collective-permute-start.7
  49.3 2.5 %gather_fusion = bf16[6,384,384]{2,1,0:T(8,128)(2,1)S(1)} fusion(bf16[7,384,384]{2,1,0:T(8,128)(2,1)} %constant_dynamic-update-slice_fusion, s32[1024]{0:T(1024)S(1)} %pad_clamp_fusion), kind=kCustom, calls=%fused_computation | custom fusion | bytes 3538968 | tf_op jit(solution)/shard_map/jit(_take)/gather | solution.py:50
  52.1 3.9 %collective-permute-done.7 = bf16[1,384,384]{2,1,0:T(8,128)(2,1)} collective-permute-done((bf16[1,384,384]{2,1,0:T(8,128)(2,1)}, bf16[1,384,384]{2,1,0:T(8,128)(2,1)}, u32[]{:S(2)}, u32[]{:S(2)}) %collective-permute-start.7) | collective-permute-done | bytes 294944 | tf_op jit(solution)/shard_map/ppermute | solution.py:26
  56.0 6.3 %fusion.12 = bf16[8,384,384]{2,1,0:T(8,128)(2,1)} fusion(bf16[2,384,384]{2,1,0:T(8,128)(2,1)} %bitcast.40, bf16[6,384,384]{2,1,0:T(8,128)(2,1)} %bitcast.39, bf16[1,384,384]{2,1,0:T(8,128)(2,1)} %collective-permute-done.7, bf16[1,384,384]{2,1,0:T(8,128)(2,1)} %collective-permute-done.6, bf16[6,384,384]{2,1,0:T(8,128)(2,1)S(1)} %broadcast_select_fusion, ...), kind=kOutput, calls=%fused_computation.16 | convolution fusion | flops 1816657920 | bytes 7372800 | tf_op jit(solution)/shard_map/fc,kfm->kcm/dot_general | solution.py:61
  62.3 3.3 %copy.10 = bf16[8,384,384]{1,0,2:T(8,128)(2,1)S(1)} copy(bf16[8,384,384]{2,1,0:T(8,128)(2,1)} %fusion.12) | data formatting | bytes 4718592 | tf_op jit(solution)/shard_map/fc,kfm->kcm/dot_general | solution.py:61
  65.6 3.5 %convert_bitcast_fusion = f32[384,3,2,384]{3,1,2,0:T(4,128)} fusion(bf16[8,384,384]{1,0,2:T(8,128)(2,1)S(1)} %copy.10, f32[8]{0:T(128)S(1)} %add_convert_fusion, f32[8,2]{0,1:T(2,128)S(1)} %copy-done.1, f32[8,3]{0,1:T(4,128)S(1)} %fusion.31), kind=kOutput, calls=%fused_computation.6 | convolution fusion | flops 15040608 | bytes 5898432 | tf_op jit(solution)/shard_map/ksb,kcm->csbm/dot_general | solution.py:78
  69.1 6.2 %copy.8 = f32[384,3,2,384]{0,3,2,1:T(8,128)} copy(f32[384,3,2,384]{3,1,2,0:T(4,128)} %convert_bitcast_fusion) | data formatting | bytes 7077888 | tf_op jit(solution)/shard_map/convert_element_type | solution.py:79
  75.4 3.3 %copy.9 = f32[384,2304]{1,0:T(8,128)S(1)} copy(f32[384,2304]{0,1:T(8,128)} %bitcast.38) | data formatting | bytes 7077888 | tf_op jit(solution)/shard_map/convert_element_type | solution.py:79
  78.7 2.2 %fusion = bf16[768,2304]{1,0:T(8,128)(2,1)} fusion(f32[384,2304]{1,0:T(8,128)S(1)} %copy.9, f32[768]{0:T(1024)S(1)} %mul.42), kind=kLoop, calls=%fused_computation.3 | loop fusion | flops 3538944 | bytes 7080960 | tf_op jit(solution)/shard_map/convert_element_type | solution.py:83
  80.9 46.1 %reduce-scatter.2.cloned.1.call-done = bf16[96,2304]{1,0:T(8,128)(2,1)} async-done(((bf16[768,2304]{1,0:T(8,128)(2,1)}), bf16[96,2304]{1,0:T(8,128)(2,1)}) %reduce-scatter.2.cloned.1.call-update) | async-done | bytes 442384 | tf_op jit(solution)/shard_map/reduce_scatter | solution.py:82
  127.0 2.0 %convert_element_type.64 = f32[96,2304]{1,0:T(8,128)} convert(bf16[96,2304]{1,0:T(8,128)(2,1)} %reduce-scatter.2.cloned.1.call-done) | non-fusion elementwise | flops 221184 | bytes 1327104 | tf_op jit(solution)/shard_map/convert_element_type | solution.py:84
  (46 shorter events, 10.0 us)
Async XLA Ops:
  6.5 39.7 %copy-start = (bf16[1,384,384]{2,1,0:T(8,128)(2,1)S(1)}, bf16[1,384,384]{2,1,0:T(8,128)(2,1)}, u32[]{:S(2)}) copy-start(bf16[1,384,384]{2,1,0:T(8,128)(2,1)} %param.12) | copy-start | bytes 884740
  6.5 120.5 %reduce-scatter.2.cloned.1.call-start = ((), (), s32[]{:S(2)}) async-start(), calls=%async_computation.1 | async-start | bytes 3981312 | tf_op jit(solution)/shard_map/reduce_scatter | solution.py:82
  6.5 9.7 %collective-permute-start.10 = (s32[1]{0:T(128)}, s32[1]{0:T(128)}, u32[]{:S(2)}, u32[]{:S(2)}) collective-permute-start(s32[1]{0:T(128)} %param.11), channel_id=1, source_target_pairs={{7,0},{0,1},{1,2},{2,3},{3,4},{4,5},{5,6},{6,7},{15,8},{8,9},{9,10... | collective-permute-start | bytes 20 | tf_op jit(solution)/shard_map/ppermute | solution.py:15
  7.0 9.9 %collective-permute-start.11 = (s32[1]{0:T(128)}, s32[1]{0:T(128)}, u32[]{:S(2)}, u32[]{:S(2)}) collective-permute-start(s32[1]{0:T(128)} %param.11), channel_id=1, source_target_pairs={{1,0},{2,1},{3,2},{4,3},{5,4},{6,5},{7,6},{0,7},{9,8},{10,9},{11,1... | collective-permute-start | bytes 20 | tf_op jit(solution)/shard_map/ppermute | solution.py:15
  9.9 7.5 %collective-permute-start.12 = (s32[1]{0:T(128)}, s32[1]{0:T(128)}, u32[]{:S(2)}, u32[]{:S(2)}) collective-permute-start(s32[1]{0:T(128)} %param.11), channel_id=1, source_target_pairs={{2,0},{3,1},{4,2},{5,3},{6,4},{7,5},{0,6},{1,7},{10,8},{11,9},{12,... | collective-permute-start | bytes 20 | tf_op jit(solution)/shard_map/ppermute | solution.py:15
  12.2 6.1 %collective-permute-start.13 = (s32[1]{0:T(128)}, s32[1]{0:T(128)}, u32[]{:S(2)}, u32[]{:S(2)}) collective-permute-start(s32[1]{0:T(128)} %param.11), channel_id=1, source_target_pairs={{3,0},{4,1},{5,2},{6,3},{7,4},{0,5},{1,6},{2,7},{11,8},{12,9},{13,... | collective-permute-start | bytes 20 | tf_op jit(solution)/shard_map/ppermute | solution.py:15
  12.2 7.4 %collective-permute-start.8 = (s32[1]{0:T(128)}, s32[1]{0:T(128)}, u32[]{:S(2)}, u32[]{:S(2)}) collective-permute-start(s32[1]{0:T(128)} %param.11), channel_id=1, source_target_pairs={{5,0},{6,1},{7,2},{0,3},{1,4},{2,5},{3,6},{4,7},{13,8},{14,9},{15,... | collective-permute-start | bytes 20 | tf_op jit(solution)/shard_map/ppermute | solution.py:15
  16.2 5.3 %collective-permute-start.9 = (s32[1]{0:T(128)}, s32[1]{0:T(128)}, u32[]{:S(2)}, u32[]{:S(2)}) collective-permute-start(s32[1]{0:T(128)} %param.11), channel_id=1, source_target_pairs={{6,0},{7,1},{0,2},{1,3},{2,4},{3,5},{4,6},{5,7},{14,8},{15,9},{8,1... | collective-permute-start | bytes 20 | tf_op jit(solution)/shard_map/ppermute | solution.py:15
  16.9 22.2 %collective-permute-start = (bf16[1,384,384]{2,1,0:T(8,128)(2,1)}, bf16[1,384,384]{2,1,0:T(8,128)(2,1)S(1)}, u32[]{:S(2)}, u32[]{:S(2)}) collective-permute-start(bf16[1,384,384]{2,1,0:T(8,128)(2,1)} %param.12), channel_id=1, source_target_pairs={{5,0},{6,1},{7,2},{0,3},{1,4},{2,5},{3,6},{4,7},{13,8},{14,9},{15,... | collective-permute-start | bytes 884744 | tf_op jit(solution)/shard_map/ppermute | solution.py:15
  17.4 22.4 %collective-permute-start.1 = (bf16[1,384,384]{2,1,0:T(8,128)(2,1)}, bf16[1,384,384]{2,1,0:T(8,128)(2,1)S(1)}, u32[]{:S(2)}, u32[]{:S(2)}) collective-permute-start(bf16[1,384,384]{2,1,0:T(8,128)(2,1)} %param.12), channel_id=1, source_target_pairs={{6,0},{7,1},{0,2},{1,3},{2,4},{3,5},{4,6},{5,7},{14,8},{15,9},{8,1... | collective-permute-start | bytes 884744 | tf_op jit(solution)/shard_map/ppermute | solution.py:15
  18.3 26.0 %collective-permute-start.2 = (bf16[1,384,384]{2,1,0:T(8,128)(2,1)}, bf16[1,384,384]{2,1,0:T(8,128)(2,1)S(1)}, u32[]{:S(2)}, u32[]{:S(2)}) collective-permute-start(bf16[1,384,384]{2,1,0:T(8,128)(2,1)} %param.12), channel_id=1, source_target_pairs={{7,0},{0,1},{1,2},{2,3},{3,4},{4,5},{5,6},{6,7},{15,8},{8,9},{9,10... | collective-permute-start | bytes 884744 | tf_op jit(solution)/shard_map/ppermute | solution.py:15
  19.6 27.4 %collective-permute-start.3 = (bf16[1,384,384]{2,1,0:T(8,128)(2,1)}, bf16[1,384,384]{2,1,0:T(8,128)(2,1)S(1)}, u32[]{:S(2)}, u32[]{:S(2)}) collective-permute-start(bf16[1,384,384]{2,1,0:T(8,128)(2,1)} %param.12), channel_id=1, source_target_pairs={{1,0},{2,1},{3,2},{4,3},{5,4},{6,5},{7,6},{0,7},{9,8},{10,9},{11,1... | collective-permute-start | bytes 884744 | tf_op jit(solution)/shard_map/ppermute | solution.py:15
  21.6 9.2 %collective-permute-start.14 = (s32[1]{0:T(128)}, s32[1]{0:T(128)}, u32[]{:S(2)}, u32[]{:S(2)}) collective-permute-start(s32[1]{0:T(128)} %param.11), channel_id=1, source_target_pairs={{0,8},{8,16},{16,24},{1,9},{9,17},{17,25},{2,10},{10,18},{18,26},{... | collective-permute-start | bytes 20 | tf_op jit(solution)/shard_map/ppermute | solution.py:25
  30.8 5.5 %collective-permute-start.15 = (s32[1]{0:T(128)}, s32[1]{0:T(128)}, u32[]{:S(2)}, u32[]{:S(2)}) collective-permute-start(s32[1]{0:T(128)} %param.11), channel_id=1, source_target_pairs={{8,0},{16,8},{24,16},{9,1},{17,9},{25,17},{10,2},{18,10},{26,18},{... | collective-permute-start | bytes 20 | tf_op jit(solution)/shard_map/ppermute | solution.py:26
  36.3 11.5 %collective-permute-start.4 = (bf16[1,384,384]{2,1,0:T(8,128)(2,1)}, bf16[1,384,384]{2,1,0:T(8,128)(2,1)S(1)}, u32[]{:S(2)}, u32[]{:S(2)}) collective-permute-start(bf16[1,384,384]{2,1,0:T(8,128)(2,1)} %param.12), channel_id=1, source_target_pairs={{2,0},{3,1},{4,2},{5,3},{6,4},{7,5},{0,6},{1,7},{10,8},{11,9},{12,... | collective-permute-start | bytes 884744 | tf_op jit(solution)/shard_map/ppermute | solution.py:15
  39.0 9.5 %collective-permute-start.5 = (bf16[1,384,384]{2,1,0:T(8,128)(2,1)}, bf16[1,384,384]{2,1,0:T(8,128)(2,1)S(1)}, u32[]{:S(2)}, u32[]{:S(2)}) collective-permute-start(bf16[1,384,384]{2,1,0:T(8,128)(2,1)} %param.12), channel_id=1, source_target_pairs={{3,0},{4,1},{5,2},{6,3},{7,4},{0,5},{1,6},{2,7},{11,8},{12,9},{13,... | collective-permute-start | bytes 884744 | tf_op jit(solution)/shard_map/ppermute | solution.py:15
  39.8 12.3 %collective-permute-start.6 = (bf16[1,384,384]{2,1,0:T(8,128)(2,1)}, bf16[1,384,384]{2,1,0:T(8,128)(2,1)}, u32[]{:S(2)}, u32[]{:S(2)}) collective-permute-start(bf16[1,384,384]{2,1,0:T(8,128)(2,1)} %param.12), channel_id=1, source_target_pairs={{0,8},{8,16},{16,24},{1,9},{9,17},{17,25},{2,10},{10,18},{18,26},{... | collective-permute-start | bytes 884744 | tf_op jit(solution)/shard_map/ppermute | solution.py:25
  44.2 11.8 %collective-permute-start.7 = (bf16[1,384,384]{2,1,0:T(8,128)(2,1)}, bf16[1,384,384]{2,1,0:T(8,128)(2,1)}, u32[]{:S(2)}, u32[]{:S(2)}) collective-permute-start(bf16[1,384,384]{2,1,0:T(8,128)(2,1)} %param.12), channel_id=1, source_target_pairs={{8,0},{16,8},{24,16},{9,1},{17,9},{25,17},{10,2},{18,10},{26,18},{... | collective-permute-start | bytes 884744 | tf_op jit(solution)/shard_map/ppermute | solution.py:26
  62.3 3.3 %copy-start.1 = (f32[8,2]{0,1:T(2,128)S(1)}, f32[8,2]{0,1:T(2,128)}, u32[]{:S(2)}) copy-start(f32[8,2]{0,1:T(2,128)} %compare_convert_fusion) | copy-start | bytes 196
Sparse Core Ops, SparseCore 0:
  81.0 45.9 reduce-scatter.1
where the time goes:
time: 136 us
  waiting for transfers between devices  54.3 us (40%)
  local copies, waits for them, and re-layouts  25.3 us (19%)
  starting transfers between devices  23.8 us (18%)
  between operations  14.8 us (11%)
  matrix products  9.81 us (7%)
  other arithmetic  7.85 us (6%)
    reduce_scatter x1, waiting for transfers between devices, on_device(): lax.psum_scatter(spread.astype(jnp.bfloat16), 'dev', scatter_dimension=0,...  46.1 us
    ppermute x12, starting transfers between devices, passed_along(): return lax.ppermute(block, axis, route)  13.5 us
    convert_element_type x2, local copies, waits for them, and re-layouts, on_device(): partial_value = partial_value.astype(jnp.bfloat16).astype(jnp.float32)  9.53 us
    ppermute x2, waiting for transfers between devices, extended(): after = lax.ppermute(initial, axis, down)  8.1 us
    ppermute x2, starting transfers between devices, extended(): before = lax.ppermute(last, axis, up)  7.68 us
    dot_general x1, matrix products, on_device(): jnp.einsum('fc,kfm->kcm', prolong[0], qmat, preferred_element_type=jnp.fl...  6.32 us
    unnamed x10, local copies, waits for them, and re-layouts  4.47 us
    concatenate x1, local copies, waits for them, and re-layouts, on_device(): window_aggs = jnp.concatenate(agg_list, axis=0)  3.89 us
  transfers between devices with their start and end apart: 17, of which 3 were waited for; matrix products, arithmetic and copies ran while one was open for 12% of the time, Pallas kernels for 0%

commit v1 on v0

--- a/solution.py
+++ b/solution.py
@@ -1,12 +1,19 @@
 import jax
 import jax.numpy as jnp
 from jax import lax
+from jax.experimental import pallas as pl
+from jax.experimental.pallas import tpu as pltpu
 from jax.sharding import PartitionSpec as P
 
 NB = 384
 SLOTS = 6
 REACH = 3
 COARSE = 2
+QUARTER = NB // 4
+META = 16
+LANES = (0, 1, 2, 3, 5, 6, 7)
+F32 = jnp.float32
+BF16 = jnp.bfloat16
 
 
 def passed_along(block, axis, distance):
@@ -28,7 +35,7 @@
     return array
 
 
-def on_device(stiff_rows, stiff_iface, columns, live_count, aggregate, prolong):
+def on_any_slab(stiff_rows, stiff_iface, columns, live_count, aggregate, prolong):
     dev_count = lax.axis_size("dev")
     grp_count = lax.axis_size("grp")
     group_at = lax.axis_index("grp")
@@ -55,33 +62,236 @@
     )
     blocks = jnp.concatenate([panels, slab_blocks[0:1], slab_blocks[2:3]], axis=0)
     stiff = jnp.concatenate([stiff_rows[0], stiff_iface[0]], axis=0)
-    qmat = jnp.einsum("kfg,kgm->kfm", stiff, blocks, preferred_element_type=jnp.float32).astype(
-        jnp.bfloat16
-    )
-    contrib = jnp.einsum("fc,kfm->kcm", prolong[0], qmat, preferred_element_type=jnp.float32)
-    low_agg = slab_aggs[0]
-    up_agg = slab_aggs[2]
-    targets = jnp.concatenate([column_aggs, low_agg[None], up_agg[None]])
+    qmat = jnp.einsum("kfg,kgm->kfm", stiff, blocks, preferred_element_type=F32).astype(BF16)
+    contrib = jnp.einsum("fc,kfm->kcm", prolong[0], qmat, preferred_element_type=F32)
+    targets = jnp.concatenate([column_aggs, slab_aggs[0][None], slab_aggs[2][None]])
     weights = jnp.concatenate(
         [
-            (jnp.arange(SLOTS, dtype=jnp.int32) < live_count[0]).astype(jnp.float32),
-            (group_at > 0).astype(jnp.float32)[None],
-            (group_at < grp_count - 1).astype(jnp.float32)[None],
+            (jnp.arange(SLOTS, dtype=jnp.int32) < live_count[0]).astype(F32),
+            (group_at > 0).astype(F32)[None],
+            (group_at < grp_count - 1).astype(F32)[None],
         ]
     )
     sides = jnp.concatenate([jnp.ones((SLOTS,), jnp.int32), jnp.array([0, 2], jnp.int32)])
-    side_hot = (sides[:, None] == jnp.arange(3, dtype=jnp.int32)[None, :]).astype(jnp.float32)
-    block_hot = (targets[:, None] == jnp.arange(COARSE, dtype=jnp.int32)[None, :]).astype(
-        jnp.float32
-    )
+    side_hot = (sides[:, None] == jnp.arange(3, dtype=jnp.int32)[None, :]).astype(F32)
+    block_hot = (targets[:, None] == jnp.arange(COARSE, dtype=jnp.int32)[None, :]).astype(F32)
     placing = side_hot[:, :, None] * block_hot[:, None, :] * weights[:, None, None]
     partial_value = jnp.einsum("ksb,kcm->csbm", placing, contrib).reshape(NB, 3 * COARSE * NB)
-    partial_value = partial_value.astype(jnp.bfloat16).astype(jnp.float32)
-    own_hot = (jnp.arange(COARSE, dtype=jnp.int32) == aggregate[0]).astype(jnp.float32)
+    partial_value = partial_value.astype(BF16).astype(F32)
+    own_hot = (jnp.arange(COARSE, dtype=jnp.int32) == aggregate[0]).astype(F32)
     spread = (own_hot[:, None, None] * partial_value[None]).reshape(COARSE * NB, 3 * COARSE * NB)
     return lax.psum_scatter(
-        spread.astype(jnp.bfloat16), "dev", scatter_dimension=0, tiled=True
-    ).astype(jnp.float32)
+        spread.astype(BF16), "dev", scatter_dimension=0, tiled=True
+    ).astype(F32)
+
+
+def dot(a, b):
+    return jnp.dot(a, b, preferred_element_type=F32)
+
+
+def left_kernel(columns, live, prolong, rows, iface, left, left_iface):
+    place = lax.axis_index("dev")
+    turned = prolong[0].T
+    for s in range(2):
+        left_iface[s] = dot(turned, iface[0, s]).astype(BF16)
+    for k in range(SLOTS):
+
+        @pl.when(k < live[0])
+        def _():
+            left[columns[0, k] ^ place] = dot(turned, rows[0, k]).astype(BF16)
+
+
+def iface_kernel(left_iface, below, above, out0, out1, out2, out3, held):
+    quarter = lax.axis_index("dev") % 4
+    for s, block in enumerate((below, above)):
+        held[s] = dot(left_iface[s], block[:NB]).astype(BF16)
+    for t, out in enumerate((out0, out1, out2, out3)):
+        start = pl.multiple_of((quarter ^ t) * QUARTER, QUARTER)
+        for s, block in enumerate((below, above)):
+            out[s * QUARTER : (s + 1) * QUARTER] = held[s, pl.ds(start, QUARTER)]
+            out[2 * QUARTER + s * META : 2 * QUARTER + (s + 1) * META] = block[NB:]
+
+
+def slab_kernel(columns, live, left, b0, b1, b2, b3, b5, b6, b7, out0, out1, out2, out3, held):
+    place = lax.axis_index("dev")
+    quarter = place % 4
+    held[...] = jnp.zeros_like(held)
+    for t, block in zip(LANES, (b0, b1, b2, b3, b5, b6, b7)):
+        present = jnp.bool_(False)
+        for k in range(SLOTS):
+            present = present | ((k < live[0]) & ((columns[0, k] ^ place) == t))
+
+        @pl.when(present)
+        def _():
+            value = dot(left[t], block[:NB])
+            upper = block[NB : NB + 1].astype(F32)
+            held[0] += value * (1.0 - upper)
+            held[1] += value * upper
+
+    for t, out in enumerate((out0, out1, out2, out3)):
+        start = pl.multiple_of((quarter ^ t) * QUARTER, QUARTER)
+        for b in range(COARSE):
+            out[b * QUARTER : (b + 1) * QUARTER] = held[b, pl.ds(start, QUARTER)].astype(BF16)
+
+
+def summed(own, other, parts, marks, shape_of, kept, sent):
+    for column, pieces in enumerate(shape_of(parts)):
+        keep, send = None, None
+        for value, mark in zip(pieces, marks):
+            here = value * (own * mark + other * (1.0 - mark))
+            there = value * (other * mark + own * (1.0 - mark))
+            keep = here if keep is None else keep + here
+            send = there if send is None else send + there
+        kept[:, column * NB : (column + 1) * NB] = keep
+        sent[:, column * NB : (column + 1) * NB] = send.astype(BF16)
+
+
+def own_side():
+    upper = (lax.axis_index("dev") // 4).astype(F32)
+    return upper, 1.0 - upper
+
+
+def iface_sum_kernel(v0, v1, v2, v3, m0, m1, m2, m3, kept, sent):
+    own, other = own_side()
+
+    def shape_of(parts):
+        for s in range(2):
+            for b in range(COARSE):
+                pieces = []
+                for v in parts:
+                    mark = v[2 * QUARTER + s * META : 2 * QUARTER + s * META + 1].astype(F32)
+                    weight = mark if b else 1.0 - mark
+                    pieces.append(v[s * QUARTER : (s + 1) * QUARTER].astype(F32) * weight)
+                yield pieces
+
+    marks = [m[0:1].astype(F32) for m in (m0, m1, m2, m3)]
+    summed(own, other, (v0, v1, v2, v3), marks, shape_of, kept, sent)
+
+
+def slab_sum_kernel(v0, v1, v2, v3, m0, m1, m2, m3, kept, sent):
+    own, other = own_side()
+
+    def shape_of(parts):
+        for b in range(COARSE):
+            yield [v[b * QUARTER : (b + 1) * QUARTER].astype(F32) for v in parts]
+
+    marks = [m[0:1].astype(F32) for m in (m0, m1, m2, m3)]
+    summed(own, other, (v0, v1, v2, v3), marks, shape_of, kept, sent)
+
+
+def last_kernel(kept_iface, got_iface, kept_slab, got_slab, out):
+    wide = COARSE * NB
+    out[:, :wide] = kept_iface[:, :wide] + got_iface[:, :wide].astype(F32)
+    out[:, wide : 2 * wide] = kept_slab[...] + got_slab[...].astype(F32)
+    out[:, 2 * wide :] = kept_iface[:, wide:] + got_iface[:, wide:].astype(F32)
+
+
+def whole():
+    return pl.BlockSpec(memory_space=pltpu.VMEM)
+
+
+def scalars():
+    return pl.BlockSpec(memory_space=pltpu.SMEM)
+
+
+def mark_rows():
+    return pl.BlockSpec((META, NB), lambda i: (NB // META, 0))
+
+
+def cost(dots, size):
+    return pl.CostEstimate(flops=2 * dots * NB**3, bytes_accessed=size, transcendentals=0)
+
+
+def on_square(stiff_rows, stiff_iface, columns, live_count, aggregate, prolong):
+    groups = lax.axis_size("grp")
+    up = [(i, i + 1) for i in range(groups - 1)]
+    down = [(j, i) for i, j in up]
+
+    def hop(block, turn):
+        return lax.ppermute(block, "dev", [(i, i ^ turn) for i in range(8)])
+
+    tail = jnp.broadcast_to(aggregate[0].astype(BF16), (META, NB))
+    mine = jnp.concatenate([prolong[0], tail], axis=0)
+    below = lax.ppermute(mine, "grp", up)
+    above = lax.ppermute(mine, "grp", down)
+    b6 = hop(mine, 6)
+    b2 = hop(mine, 2)
+    b5 = hop(mine, 5)
+    b1 = hop(mine, 1)
+    b3 = hop(b2, 1)
+    b7 = hop(b6, 1)
+
+    left, left_iface = pl.pallas_call(
+        left_kernel,
+        out_shape=(
+            jax.ShapeDtypeStruct((8, NB, NB), BF16),
+            jax.ShapeDtypeStruct((2, NB, NB), BF16),
+        ),
+        in_specs=[scalars(), scalars(), whole(), whole(), whole()],
+        out_specs=(whole(), whole()),
+        cost_estimate=cost(8, 20 * NB * NB),
+        name="left",
+    )(columns, live_count, prolong, stiff_rows, stiff_iface)
+
+    part = jax.ShapeDtypeStruct((2 * QUARTER + 2 * META, NB), BF16)
+    ti = pl.pallas_call(
+        iface_kernel,
+        out_shape=(part,) * 4,
+        in_specs=[whole()] * 3,
+        out_specs=(whole(),) * 4,
+        scratch_shapes=[pltpu.VMEM((2, NB, NB), BF16)],
+        cost_estimate=cost(2, 8 * NB * NB),
+        name="iface",
+    )(left_iface, below, above)
+    ri = [ti[0]] + [hop(ti[t], t) for t in (1, 2, 3)]
+
+    part = jax.ShapeDtypeStruct((2 * QUARTER, NB), BF16)
+    ts = pl.pallas_call(
+        slab_kernel,
+        out_shape=(part,) * 4,
+        in_specs=[scalars(), scalars()] + [whole()] * 8,
+        out_specs=(whole(),) * 4,
+        scratch_shapes=[pltpu.VMEM((COARSE, NB, NB), F32)],
+        cost_estimate=cost(6, 16 * NB * NB),
+        name="slab",
+    )(columns, live_count, left, mine, b1, b2, b3, b5, b6, b7)
+    rs = [ts[0]] + [hop(ts[t], t) for t in (1, 2, 3)]
+
+    marks = (mine, b1, b2, b3)
+    kept_iface, sent_iface = pl.pallas_call(
+        iface_sum_kernel,
+        out_shape=(
+            jax.ShapeDtypeStruct((QUARTER, 4 * NB), F32),
+            jax.ShapeDtypeStruct((QUARTER, 4 * NB), BF16),
+        ),
+        grid=(1,),
+        in_specs=[whole()] * 4 + [mark_rows()] * 4,
+        out_specs=(whole(), whole()),
+        cost_estimate=cost(0, 8 * NB * NB),
+        name="iface_sum",
+    )(*ri, *marks)
+    got_iface = hop(sent_iface, 4)
+    kept_slab, sent_slab = pl.pallas_call(
+        slab_sum_kernel,
+        out_shape=(
+            jax.ShapeDtypeStruct((QUARTER, 2 * NB), F32),
+            jax.ShapeDtypeStruct((QUARTER, 2 * NB), BF16),
+        ),
+        grid=(1,),
+        in_specs=[whole()] * 4 + [mark_rows()] * 4,
+        out_specs=(whole(), whole()),
+        cost_estimate=cost(0, 4 * NB * NB),
+        name="slab_sum",
+    )(*rs, *marks)
+    got_slab = hop(sent_slab, 4)
+    return pl.pallas_call(
+        last_kernel,
+        out_shape=jax.ShapeDtypeStruct((QUARTER, 6 * NB), F32),
+        in_specs=[whole()] * 4,
+        out_specs=whole(),
+        cost_estimate=cost(0, 10 * NB * NB),
+        name="last",
+    )(kept_iface, got_iface, kept_slab, got_slab)
 
 
 def solution(mesh):
@@ -94,6 +304,7 @@
         P(("grp", "dev"), None, None),
     )
     out_specs = P(("grp", "dev"), None)
+    on_device = on_square if mesh.shape["dev"] == 8 else on_any_slab
     return jax.shard_map(
         on_device, mesh=mesh, in_specs=in_specs, out_specs=out_specs, check_vma=False
     )

time: 136 us -> 59.4 us (0.44)
  waiting for transfers between devices: 54.3 us -> 17.4 us
  local copies, waits for them, and re-layouts: 25.3 us -> 4.59 us
  Pallas kernels: 0 us -> 20.1 us
  between operations: 14.8 us -> 1.44 us
  matrix products: 9.81 us -> 0 us
  starting transfers between devices: 23.8 us -> 15.6 us
  other arithmetic: 7.85 us -> 0 us
    reduce_scatter x1 -> x0, waiting for transfers between devices: 46.1 us -> none  [on_device(): lax.psum_scatter(spread.astype(jnp.bfloat16), 'dev', scatter_dimension=0,...]
    pallas_call x0 -> x6, Pallas kernels: none -> 20.1 us  [the longest x1 5.51 us: on_square(): pl.pallas_call(left_kernel, out_shape=(jax.ShapeDtypeStruct((8, NB, NB),...]
    dot_general x2 -> x0, matrix products: 9.81 us -> none  [the longest x1 6.32 us: on_device(): jnp.einsum('fc,kfm->kcm', prolong[0], qmat, preferred_element_type=jnp.fl...]
    convert_element_type x2 -> x0, local copies, waits for them, and re-layouts: 9.53 us -> none  [on_device(): partial_value = partial_value.astype(jnp.bfloat16).astype(jnp.float32)]
    ppermute x16, waiting for transfers between devices: 8.13 us -> 17.4 us  [the longest x14 17.4 us: hop(): return lax.ppermute(block, 'dev', [(i, i ^ turn) for i in range(8)])]
    ppermute x16, starting transfers between devices: 23.8 us -> 15.6 us  [the longest x14 10.8 us: hop(): return lax.ppermute(block, 'dev', [(i, i ^ turn) for i in range(8)])]
    convert_element_type x5 -> x0, other arithmetic: 4.76 us -> none  [the longest x1 2.2 us: on_device(): spread.astype(jnp.bfloat16)]
    concatenate x3 -> x1, local copies, waits for them, and re-layouts: 4.74 us -> 0.99 us  [on_square(): mine = jnp.concatenate([prolong[0], tail], axis=0)]
  transfers between devices with their start and end apart: 17 -> 16, of which waited for: 3 -> 6; matrix products, arithmetic and copies ran while one was open for 12% -> 0% of each run, Pallas kernels for 0% -> 30%
where the time goes in v1:
time: 59.4 us; the launch traced here: 59.1 us
  Pallas kernels  20.1 us (34%)
  waiting for transfers between devices  17.4 us (29%)
  starting transfers between devices  15.6 us (26%)
  local copies, waits for them, and re-layouts  4.59 us (8%)
  between operations  1.44 us (2%)
    ppermute x14, waiting for transfers between devices, hop(): return lax.ppermute(block, 'dev', [(i, i ^ turn) for i in range(8)])  17.4 us
    ppermute x14, starting transfers between devices, hop(): return lax.ppermute(block, 'dev', [(i, i ^ turn) for i in range(8)])  10.8 us
    pallas_call x1, Pallas kernels, on_square(): pl.pallas_call(left_kernel, out_shape=(jax.ShapeDtypeStruct((8, NB, NB),...  5.51 us
    pallas_call x1, Pallas kernels, on_square(): pl.pallas_call(slab_kernel, out_shape=(part,) * 4, in_specs=[scalars(), s...  5.06 us
    unnamed x34, local copies, waits for them, and re-layouts  3.59 us
    ppermute x1, starting transfers between devices, on_square(): below = lax.ppermute(mine, 'grp', up)  3.49 us
    pallas_call x1, Pallas kernels, on_square(): pl.pallas_call(iface_kernel, out_shape=(part,) * 4, in_specs=[whole()] *...  2.64 us
    pallas_call x1, Pallas kernels, on_square(): pl.pallas_call(iface_sum_kernel, out_shape=(jax.ShapeDtypeStruct((QUARTER...  2.56 us
  transfers between devices with their start and end apart: 16, of which 6 were waited for; matrix products, arithmetic and copies ran while one was open for 0% of the time, Pallas kernels for 30%

profile of v1, /device:TPU:0, one launch (start us, length us, event | category | flops | bytes accessed | tf_op | source)
XLA Modules:
  0.0 59.1 jit_solution(11510606868554390342)
XLA Ops:
  0.7 1.0 %concatenate.3.m0.b0 = bf16[400,384]{1,0:T(8,128)(2,1)S(1)} pad(bf16[384,384]{1,0:T(8,128)(2,1)} %bitcast.2, bf16[]{:T(256)} %bitcast.1), padding=0_16x0_0 | pad | bytes 602114 | tf_op jit(solution)/shard_map/concatenate | solution.py:214
  1.7 3.0 %collective-permute-start.6 = (bf16[400,384]{1,0:T(8,128)(2,1)S(1)}, bf16[400,384]{1,0:T(8,128)(2,1)S(1)}, u32[]{:S(2)}, u32[]{:S(2)}) collective-permute-start(bf16[400,384]{1,0:T(8,128)(2,1)S(1)} %concatenate.3.m0.b0), channel_id=1, source_target_pairs={{0,2},{1,3},{2,0},{3,1},{4,6},{5,7},{6,4},{7,5},{8,10},{9,11},{10,... | collective-permute-start | bytes 921608 | tf_op jit(solution)/shard_map/ppermute | solution.py:211
  4.7 1.5 %collective-permute-start.10 = (bf16[400,384]{1,0:T(8,128)(2,1)S(1)}, bf16[400,384]{1,0:T(8,128)(2,1)S(1)}, u32[]{:S(2)}, u32[]{:S(2)}) collective-permute-start(bf16[400,384]{1,0:T(8,128)(2,1)S(1)} %concatenate.3.m0.b0), channel_id=1, source_target_pairs={{0,6},{1,7},{2,4},{3,5},{4,2},{5,3},{6,0},{7,1},{8,14},{9,15},{10,... | collective-permute-start | bytes 921608 | tf_op jit(solution)/shard_map/ppermute | solution.py:211
  6.2 3.5 %collective-permute-start = (bf16[400,384]{1,0:T(8,128)(2,1)S(1)}, bf16[400,384]{1,0:T(8,128)(2,1)S(1)}, u32[]{:S(2)}, u32[]{:S(2)}) collective-permute-start(bf16[400,384]{1,0:T(8,128)(2,1)S(1)} %concatenate.3.m0.b0), channel_id=1, source_target_pairs={{0,8},{8,16},{16,24},{1,9},{9,17},{17,25},{2,10},{10,18},{18,26},{... | collective-permute-start | bytes 921608 | tf_op jit(solution)/shard_map/ppermute | solution.py:215
  9.7 1.3 %collective-permute-start.1 = (bf16[400,384]{1,0:T(8,128)(2,1)S(1)}, bf16[400,384]{1,0:T(8,128)(2,1)S(1)}, u32[]{:S(2)}, u32[]{:S(2)}) collective-permute-start(bf16[400,384]{1,0:T(8,128)(2,1)S(1)} %concatenate.3.m0.b0), channel_id=1, source_target_pairs={{8,0},{16,8},{24,16},{9,1},{17,9},{25,17},{10,2},{18,10},{26,18},{... | collective-permute-start | bytes 921608 | tf_op jit(solution)/shard_map/ppermute | solution.py:216
  11.0 1.7 %collective-permute-done.6.m2.b2 = bf16[400,384]{1,0:T(8,128)(2,1)S(1)} collective-permute-done((bf16[400,384]{1,0:T(8,128)(2,1)S(1)}, bf16[400,384]{1,0:T(8,128)(2,1)S(1)}, u32[]{:S(2)}, u32[]{:S(2)}) %collective-permute-start.6) | collective-permute-done | bytes 307232 | tf_op jit(solution)/shard_map/ppermute | solution.py:211
  12.8 7.1 %collective-permute-done.10.b6 = bf16[400,384]{1,0:T(8,128)(2,1)S(1)} collective-permute-done((bf16[400,384]{1,0:T(8,128)(2,1)S(1)}, bf16[400,384]{1,0:T(8,128)(2,1)S(1)}, u32[]{:S(2)}, u32[]{:S(2)}) %collective-permute-start.10) | collective-permute-done | bytes 307232 | tf_op jit(solution)/shard_map/ppermute | solution.py:211
  21.0 5.5 %left.1 = (bf16[8,384,384]{2,1,0:T(8,128)(2,1)}, bf16[2,384,384]{2,1,0:T(8,128)(2,1)}) custom-call(s32[1,6]{1,0:T(1,128)} %columns.3, s32[1]{0:T(128)S(6)} %copy.7.live, bf16[1,384,384]{2,1,0:T(8,128)(2,1)} %prolong.1, bf16[1,6,384,384]{3,2,1,0:T(8,128)(2,1)} %rows.1, bf16[1,2,384,384]{3,2,1,0:T(8,128)(2,1)} %iface.2), custom_call_target="tpu_custom_call" | custom-call | flops 905969664 | bytes 2949120 | tf_op jit(solution)/shard_map/left/pallas_call | solution.py:224
  26.5 0.7 %copy-done.5 = bf16[400,384]{1,0:T(8,128)(2,1)} copy-done((bf16[400,384]{1,0:T(8,128)(2,1)}, bf16[400,384]{1,0:T(8,128)(2,1)S(1)}, u32[]{:S(2)}) %copy-start.5) | copy-done | bytes 307224
  27.2 2.6 %iface.3 = (bf16[224,384]{1,0:T(8,128)(2,1)}, bf16[224,384]{1,0:T(8,128)(2,1)}, bf16[224,384]{1,0:T(8,128)(2,1)}, bf16[224,384]{1,0:T(8,128)(2,1)}) custom-call(bf16[2,384,384]{2,1,0:T(8,128)(2,1)} %get-tuple-element.19.left_iface, bf16[400,384]{1,0:T(8,128)(2,1)} %copy-done.4, bf16[400,384]{1,0:T(8,128)(2,1)} %copy-done.5), custom_call_target="tpu_custom_call" | custom-call | flops 226492416 | bytes 1179648 | tf_op jit(solution)/shard_map/iface/pallas_call | solution.py:237
  30.0 0.9 %collective-permute-start.3 = (bf16[224,384]{1,0:T(8,128)(2,1)}, bf16[224,384]{1,0:T(8,128)(2,1)S(1)}, u32[]{:S(2)}, u32[]{:S(2)}) collective-permute-start(bf16[224,384]{1,0:T(8,128)(2,1)} %get-tuple-element.22), channel_id=1, source_target_pairs={{0,2},{1,3},{2,0},{3,1},{4,6},{5,7},{6,4},{7,5},{8,10},{9,11},{10,... | collective-permute-start | bytes 516104 | tf_op jit(solution)/shard_map/ppermute | solution.py:211
  30.9 0.9 %collective-permute-start.4 = (bf16[224,384]{1,0:T(8,128)(2,1)}, bf16[224,384]{1,0:T(8,128)(2,1)S(1)}, u32[]{:S(2)}, u32[]{:S(2)}) collective-permute-start(bf16[224,384]{1,0:T(8,128)(2,1)} %get-tuple-element.23), channel_id=1, source_target_pairs={{0,3},{1,2},{2,1},{3,0},{4,7},{5,6},{6,5},{7,4},{8,11},{9,10},{10,... | collective-permute-start | bytes 516104 | tf_op jit(solution)/shard_map/ppermute | solution.py:211
  31.8 0.7 %copy-done.3 = bf16[400,384]{1,0:T(8,128)(2,1)} copy-done((bf16[400,384]{1,0:T(8,128)(2,1)}, bf16[400,384]{1,0:T(8,128)(2,1)S(1)}, u32[]{:S(2)}) %copy-start.3) | copy-done | bytes 307224
  32.6 5.1 %slab.1 = (bf16[192,384]{1,0:T(8,128)(2,1)}, bf16[192,384]{1,0:T(8,128)(2,1)}, bf16[192,384]{1,0:T(8,128)(2,1)}, bf16[192,384]{1,0:T(8,128)(2,1)}) custom-call(s32[1,6]{1,0:T(1,128)} %columns.3, s32[1]{0:T(128)S(6)} %copy.7.live, bf16[8,384,384]{2,1,0:T(8,128)(2,1)} %get-tuple-element.26.left, bf16[400,384]{1,0:T(8,128)(2,1)} %copy-done, ...), custom_call_target="tpu_custom_call" | custom-call | flops 679477248 | bytes 2359296 | tf_op jit(solution)/shard_map/slab/pallas_call | solution.py:249
  38.2 1.3 %collective-permute-start.14 = (bf16[192,384]{1,0:T(8,128)(2,1)}, bf16[192,384]{1,0:T(8,128)(2,1)S(1)}, u32[]{:S(2)}, u32[]{:S(2)}) collective-permute-start(bf16[192,384]{1,0:T(8,128)(2,1)} %get-tuple-element.30), channel_id=1, source_target_pairs={{0,3},{1,2},{2,1},{3,0},{4,7},{5,6},{6,5},{7,4},{8,11},{9,10},{10,... | collective-permute-start | bytes 442376 | tf_op jit(solution)/shard_map/ppermute | solution.py:211
  40.7 2.6 %iface_sum.1 = (f32[96,1536]{1,0:T(8,128)}, bf16[96,1536]{1,0:T(8,128)(2,1)}) custom-call(bf16[224,384]{1,0:T(8,128)(2,1)} %get-tuple-element.20.v0, bf16[224,384]{1,0:T(8,128)(2,1)} %copy-done.10, bf16[224,384]{1,0:T(8,128)(2,1)} %copy-done.11, bf16[224,384]{1,0:T(8,128)(2,1)} %copy-done.12, bf16[400,384]{1,0:T(8,128)(2,1)} %copy-done, ...), custom_call_target="tpu_custom_call" | custom-call | bytes 1179648 | tf_op jit(solution)/shard_map/iface_sum/pallas_call | solution.py:261
  43.2 0.8 %collective-permute-start.8 = (bf16[96,1536]{1,0:T(8,128)(2,1)}, bf16[96,1536]{1,0:T(8,128)(2,1)S(1)}, u32[]{:S(2)}, u32[]{:S(2)}) collective-permute-start(bf16[96,1536]{1,0:T(8,128)(2,1)} %get-tuple-element.25), channel_id=1, source_target_pairs={{0,4},{1,5},{2,6},{3,7},{4,0},{5,1},{6,2},{7,3},{8,12},{9,13},{10,... | collective-permute-start | bytes 884744 | tf_op jit(solution)/shard_map/ppermute | solution.py:211
  44.1 0.9 %collective-permute-done.13.v2 = bf16[192,384]{1,0:T(8,128)(2,1)S(1)} collective-permute-done((bf16[192,384]{1,0:T(8,128)(2,1)}, bf16[192,384]{1,0:T(8,128)(2,1)S(1)}, u32[]{:S(2)}, u32[]{:S(2)}) %collective-permute-start.13) | collective-permute-done | bytes 147488 | tf_op jit(solution)/shard_map/ppermute | solution.py:211
  45.0 1.4 %collective-permute-done.14.v3 = bf16[192,384]{1,0:T(8,128)(2,1)S(1)} collective-permute-done((bf16[192,384]{1,0:T(8,128)(2,1)}, bf16[192,384]{1,0:T(8,128)(2,1)S(1)}, u32[]{:S(2)}, u32[]{:S(2)}) %collective-permute-start.14) | collective-permute-done | bytes 147488 | tf_op jit(solution)/shard_map/ppermute | solution.py:211
  46.4 0.7 %copy-done.15 = bf16[192,384]{1,0:T(8,128)(2,1)} copy-done((bf16[192,384]{1,0:T(8,128)(2,1)}, bf16[192,384]{1,0:T(8,128)(2,1)S(1)}, u32[]{:S(2)}) %copy-start.15) | copy-done | bytes 147480
  47.1 2.1 %slab_sum.1 = (f32[96,768]{1,0:T(8,128)}, bf16[96,768]{1,0:T(8,128)(2,1)}) custom-call(bf16[192,384]{1,0:T(8,128)(2,1)} %get-tuple-element.27.v0, bf16[192,384]{1,0:T(8,128)(2,1)} %copy-done.13, bf16[192,384]{1,0:T(8,128)(2,1)} %copy-done.14, bf16[192,384]{1,0:T(8,128)(2,1)} %copy-done.15, bf16[400,384]{1,0:T(8,128)(2,1)} %copy-done, ...), custom_call_target="tpu_custom_call" | custom-call | bytes 589824 | tf_op jit(solution)/shard_map/slab_sum/pallas_call | solution.py:274
  49.2 1.2 %collective-permute-start.15 = (bf16[96,768]{1,0:T(8,128)(2,1)}, bf16[96,768]{1,0:T(8,128)(2,1)S(1)}, u32[]{:S(2)}, u32[]{:S(2)}) collective-permute-start(bf16[96,768]{1,0:T(8,128)(2,1)} %get-tuple-element.32), channel_id=1, source_target_pairs={{0,4},{1,5},{2,6},{3,7},{4,0},{5,1},{6,2},{7,3},{8,12},{9,13},{10,... | collective-permute-start | bytes 442376 | tf_op jit(solution)/shard_map/ppermute | solution.py:211
  50.3 5.8 %collective-permute-done.15.got_slab = bf16[96,768]{1,0:T(8,128)(2,1)S(1)} collective-permute-done((bf16[96,768]{1,0:T(8,128)(2,1)}, bf16[96,768]{1,0:T(8,128)(2,1)S(1)}, u32[]{:S(2)}, u32[]{:S(2)}) %collective-permute-start.15) | collective-permute-done | bytes 147488 | tf_op jit(solution)/shard_map/ppermute | solution.py:211
  56.9 2.2 %last.1 = f32[96,2304]{1,0:T(8,128)} custom-call(f32[96,1536]{1,0:T(8,128)} %get-tuple-element.24.kept_iface, bf16[96,1536]{1,0:T(8,128)(2,1)} %copy-done.9, f32[96,768]{1,0:T(8,128)} %get-tuple-element.31.kept_slab, bf16[96,768]{1,0:T(8,128)(2,1)} %copy-done.16), custom_call_target="tpu_custom_call" | custom-call | bytes 1474560 | tf_op jit(solution)/shard_map/last/pallas_call | solution.py:287
  (49 shorter events, 3.4 us)
Async XLA Ops:
  1.7 30.1 %copy-start = (bf16[400,384]{1,0:T(8,128)(2,1)}, bf16[400,384]{1,0:T(8,128)(2,1)S(1)}, u32[]{:S(2)}) copy-start(bf16[400,384]{1,0:T(8,128)(2,1)S(1)} %concatenate.3.m0.b0) | copy-start | bytes 921604
  1.7 11.1 %collective-permute-start.6 = (bf16[400,384]{1,0:T(8,128)(2,1)S(1)}, bf16[400,384]{1,0:T(8,128)(2,1)S(1)}, u32[]{:S(2)}, u32[]{:S(2)}) collective-permute-start(bf16[400,384]{1,0:T(8,128)(2,1)S(1)} %concatenate.3.m0.b0), channel_id=1, source_target_pairs={{0,2},{1,3},{2,0},{3,1},{4,6},{5,7},{6,4},{7,5},{8,10},{9,11},{10,... | collective-permute-start | bytes 921608 | tf_op jit(solution)/shard_map/ppermute | solution.py:211
  4.7 15.2 %collective-permute-start.10 = (bf16[400,384]{1,0:T(8,128)(2,1)S(1)}, bf16[400,384]{1,0:T(8,128)(2,1)S(1)}, u32[]{:S(2)}, u32[]{:S(2)}) collective-permute-start(bf16[400,384]{1,0:T(8,128)(2,1)S(1)} %concatenate.3.m0.b0), channel_id=1, source_target_pairs={{0,6},{1,7},{2,4},{3,5},{4,2},{5,3},{6,0},{7,1},{8,14},{9,15},{10,... | collective-permute-start | bytes 921608 | tf_op jit(solution)/shard_map/ppermute | solution.py:211
  6.2 13.7 %collective-permute-start = (bf16[400,384]{1,0:T(8,128)(2,1)S(1)}, bf16[400,384]{1,0:T(8,128)(2,1)S(1)}, u32[]{:S(2)}, u32[]{:S(2)}) collective-permute-start(bf16[400,384]{1,0:T(8,128)(2,1)S(1)} %concatenate.3.m0.b0), channel_id=1, source_target_pairs={{0,8},{8,16},{16,24},{1,9},{9,17},{17,25},{2,10},{10,18},{18,26},{... | collective-permute-start | bytes 921608 | tf_op jit(solution)/shard_map/ppermute | solution.py:215
  9.7 16.9 %collective-permute-start.1 = (bf16[400,384]{1,0:T(8,128)(2,1)S(1)}, bf16[400,384]{1,0:T(8,128)(2,1)S(1)}, u32[]{:S(2)}, u32[]{:S(2)}) collective-permute-start(bf16[400,384]{1,0:T(8,128)(2,1)S(1)} %concatenate.3.m0.b0), channel_id=1, source_target_pairs={{8,0},{16,8},{24,16},{9,1},{17,9},{25,17},{10,2},{18,10},{26,18},{... | collective-permute-start | bytes 921608 | tf_op jit(solution)/shard_map/ppermute | solution.py:216
  11.0 19.0 %collective-permute-start.5 = (bf16[400,384]{1,0:T(8,128)(2,1)S(1)}, bf16[400,384]{1,0:T(8,128)(2,1)S(1)}, u32[]{:S(2)}, u32[]{:S(2)}) collective-permute-start(bf16[400,384]{1,0:T(8,128)(2,1)S(1)} %concatenate.3.m0.b0), channel_id=1, source_target_pairs={{0,1},{1,0},{2,3},{3,2},{4,5},{5,4},{6,7},{7,6},{8,9},{9,8},{10,11... | collective-permute-start | bytes 921608 | tf_op jit(solution)/shard_map/ppermute | solution.py:211
  12.8 19.0 %copy-start.1 = (bf16[400,384]{1,0:T(8,128)(2,1)}, bf16[400,384]{1,0:T(8,128)(2,1)S(1)}, u32[]{:S(2)}) copy-start(bf16[400,384]{1,0:T(8,128)(2,1)S(1)} %collective-permute-done.6.m2.b2) | copy-start | bytes 921604
  12.8 18.1 %collective-permute-start.9 = (bf16[400,384]{1,0:T(8,128)(2,1)S(1)}, bf16[400,384]{1,0:T(8,128)(2,1)S(1)}, u32[]{:S(2)}, u32[]{:S(2)}) collective-permute-start(bf16[400,384]{1,0:T(8,128)(2,1)S(1)} %concatenate.3.m0.b0), channel_id=1, source_target_pairs={{0,5},{1,4},{2,7},{3,6},{4,1},{5,0},{6,3},{7,2},{8,13},{9,12},{10,... | collective-permute-start | bytes 921608 | tf_op jit(solution)/shard_map/ppermute | solution.py:211
  19.8 12.0 %copy-start.6 = (bf16[400,384]{1,0:T(8,128)(2,1)}, bf16[400,384]{1,0:T(8,128)(2,1)S(1)}, u32[]{:S(2)}) copy-start(bf16[400,384]{1,0:T(8,128)(2,1)S(1)} %collective-permute-done.10.b6) | copy-start | bytes 921604
  19.8 11.9 %collective-permute-start.7 = (bf16[400,384]{1,0:T(8,128)(2,1)S(1)}, bf16[400,384]{1,0:T(8,128)(2,1)S(1)}, u32[]{:S(2)}, u32[]{:S(2)}) collective-permute-start(bf16[400,384]{1,0:T(8,128)(2,1)S(1)} %collective-permute-done.6.m2.b2), channel_id=1, source_target_pairs={{0,1},{1,0},{2,3},{3,2},{4,5},{5,4},{6,7},{7,6},{8,9},{9,8},{10,11... | collective-permute-start | bytes 921608 | tf_op jit(solution)/shard_map/ppermute | solution.py:211
  19.8 6.7 %copy-start.4 = (bf16[400,384]{1,0:T(8,128)(2,1)}, bf16[400,384]{1,0:T(8,128)(2,1)S(1)}, u32[]{:S(2)}) copy-start(bf16[400,384]{1,0:T(8,128)(2,1)S(1)} %collective-permute-done.below) | copy-start | bytes 921604
  19.9 11.9 %collective-permute-start.11 = (bf16[400,384]{1,0:T(8,128)(2,1)S(1)}, bf16[400,384]{1,0:T(8,128)(2,1)S(1)}, u32[]{:S(2)}, u32[]{:S(2)}) collective-permute-start(bf16[400,384]{1,0:T(8,128)(2,1)S(1)} %collective-permute-done.10.b6), channel_id=1, source_target_pairs={{0,1},{1,0},{2,3},{3,2},{4,5},{5,4},{6,7},{7,6},{8,9},{9,8},{10,11... | collective-permute-start | bytes 921608 | tf_op jit(solution)/shard_map/ppermute | solution.py:211
  29.9 8.4 %collective-permute-start.2 = (bf16[224,384]{1,0:T(8,128)(2,1)}, bf16[224,384]{1,0:T(8,128)(2,1)S(1)}, u32[]{:S(2)}, u32[]{:S(2)}) collective-permute-start(bf16[224,384]{1,0:T(8,128)(2,1)} %get-tuple-element.21), channel_id=1, source_target_pairs={{0,1},{1,0},{2,3},{3,2},{4,5},{5,4},{6,7},{7,6},{8,9},{9,8},{10,11... | collective-permute-start | bytes 516104 | tf_op jit(solution)/shard_map/ppermute | solution.py:211
  30.0 1.8 %copy-start.2 = (bf16[400,384]{1,0:T(8,128)(2,1)}, bf16[400,384]{1,0:T(8,128)(2,1)S(1)}, u32[]{:S(2)}) copy-start(bf16[400,384]{1,0:T(8,128)(2,1)S(1)} %collective-permute-done.5.m1.b1) | copy-start | bytes 921604
  30.0 9.5 %collective-permute-start.3 = (bf16[224,384]{1,0:T(8,128)(2,1)}, bf16[224,384]{1,0:T(8,128)(2,1)S(1)}, u32[]{:S(2)}, u32[]{:S(2)}) collective-permute-start(bf16[224,384]{1,0:T(8,128)(2,1)} %get-tuple-element.22), channel_id=1, source_target_pairs={{0,2},{1,3},{2,0},{3,1},{4,6},{5,7},{6,4},{7,5},{8,10},{9,11},{10,... | collective-permute-start | bytes 516104 | tf_op jit(solution)/shard_map/ppermute | solution.py:211
  30.9 9.1 %collective-permute-start.4 = (bf16[224,384]{1,0:T(8,128)(2,1)}, bf16[224,384]{1,0:T(8,128)(2,1)S(1)}, u32[]{:S(2)}, u32[]{:S(2)}) collective-permute-start(bf16[224,384]{1,0:T(8,128)(2,1)} %get-tuple-element.23), channel_id=1, source_target_pairs={{0,3},{1,2},{2,1},{3,0},{4,7},{5,6},{6,5},{7,4},{8,11},{9,10},{10,... | collective-permute-start | bytes 516104 | tf_op jit(solution)/shard_map/ppermute | solution.py:211
  37.6 6.4 %collective-permute-start.12 = (bf16[192,384]{1,0:T(8,128)(2,1)}, bf16[192,384]{1,0:T(8,128)(2,1)S(1)}, u32[]{:S(2)}, u32[]{:S(2)}) collective-permute-start(bf16[192,384]{1,0:T(8,128)(2,1)} %get-tuple-element.28), channel_id=1, source_target_pairs={{0,1},{1,0},{2,3},{3,2},{4,5},{5,4},{6,7},{7,6},{8,9},{9,8},{10,11... | collective-permute-start | bytes 442376 | tf_op jit(solution)/shard_map/ppermute | solution.py:211
  38.1 6.9 %collective-permute-start.13 = (bf16[192,384]{1,0:T(8,128)(2,1)}, bf16[192,384]{1,0:T(8,128)(2,1)S(1)}, u32[]{:S(2)}, u32[]{:S(2)}) collective-permute-start(bf16[192,384]{1,0:T(8,128)(2,1)} %get-tuple-element.29), channel_id=1, source_target_pairs={{0,2},{1,3},{2,0},{3,1},{4,6},{5,7},{6,4},{7,5},{8,10},{9,11},{10,... | collective-permute-start | bytes 442376 | tf_op jit(solution)/shard_map/ppermute | solution.py:211
  38.2 1.8 %copy-start.10 = (bf16[224,384]{1,0:T(8,128)(2,1)}, bf16[224,384]{1,0:T(8,128)(2,1)S(1)}, u32[]{:S(2)}) copy-start(bf16[224,384]{1,0:T(8,128)(2,1)S(1)} %collective-permute-done.2.v1) | copy-start | bytes 516100
  38.2 8.2 %collective-permute-start.14 = (bf16[192,384]{1,0:T(8,128)(2,1)}, bf16[192,384]{1,0:T(8,128)(2,1)S(1)}, u32[]{:S(2)}, u32[]{:S(2)}) collective-permute-start(bf16[192,384]{1,0:T(8,128)(2,1)} %get-tuple-element.30), channel_id=1, source_target_pairs={{0,3},{1,2},{2,1},{3,0},{4,7},{5,6},{6,5},{7,4},{8,11},{9,10},{10,... | collective-permute-start | bytes 442376 | tf_op jit(solution)/shard_map/ppermute | solution.py:211
  43.2 12.9 %collective-permute-start.8 = (bf16[96,1536]{1,0:T(8,128)(2,1)}, bf16[96,1536]{1,0:T(8,128)(2,1)S(1)}, u32[]{:S(2)}, u32[]{:S(2)}) collective-permute-start(bf16[96,1536]{1,0:T(8,128)(2,1)} %get-tuple-element.25), channel_id=1, source_target_pairs={{0,4},{1,5},{2,6},{3,7},{4,0},{5,1},{6,2},{7,3},{8,12},{9,13},{10,... | collective-permute-start | bytes 884744 | tf_op jit(solution)/shard_map/ppermute | solution.py:211
  44.1 2.3 %copy-start.13 = (bf16[192,384]{1,0:T(8,128)(2,1)}, bf16[192,384]{1,0:T(8,128)(2,1)S(1)}, u32[]{:S(2)}) copy-start(bf16[192,384]{1,0:T(8,128)(2,1)S(1)} %collective-permute-done.12.v1) | copy-start | bytes 442372
  45.0 1.4 %copy-start.14 = (bf16[192,384]{1,0:T(8,128)(2,1)}, bf16[192,384]{1,0:T(8,128)(2,1)S(1)}, u32[]{:S(2)}) copy-start(bf16[192,384]{1,0:T(8,128)(2,1)S(1)} %collective-permute-done.13.v2) | copy-start | bytes 442372
  49.2 6.9 %collective-permute-start.15 = (bf16[96,768]{1,0:T(8,128)(2,1)}, bf16[96,768]{1,0:T(8,128)(2,1)S(1)}, u32[]{:S(2)}, u32[]{:S(2)}) collective-permute-start(bf16[96,768]{1,0:T(8,128)(2,1)} %get-tuple-element.32), channel_id=1, source_target_pairs={{0,4},{1,5},{2,6},{3,7},{4,0},{5,1},{6,2},{7,3},{8,12},{9,13},{10,... | collective-permute-start | bytes 442376 | tf_op jit(solution)/shard_map/ppermute | solution.py:211
  (9 other events, 6.6 us)

commit v2 on v0

--- a/solution.py
+++ b/solution.py
@@ -1,12 +1,20 @@
 import jax
 import jax.numpy as jnp
 from jax import lax
+from jax.experimental import pallas as pl
+from jax.experimental.pallas import tpu as pltpu
 from jax.sharding import PartitionSpec as P
 
 NB = 384
 SLOTS = 6
 REACH = 3
 COARSE = 2
+QUARTER = NB // 4
+HALF = NB // 2
+META = 16
+TURNS = (0, 1, 2, 3, 5, 6, 7)
+F32 = jnp.float32
+BF16 = jnp.bfloat16
 
 
 def passed_along(block, axis, distance):
@@ -28,7 +36,7 @@
     return array
 
 
-def on_device(stiff_rows, stiff_iface, columns, live_count, aggregate, prolong):
+def on_any_slab(stiff_rows, stiff_iface, columns, live_count, aggregate, prolong):
     dev_count = lax.axis_size("dev")
     grp_count = lax.axis_size("grp")
     group_at = lax.axis_index("grp")
@@ -55,33 +63,239 @@
     )
     blocks = jnp.concatenate([panels, slab_blocks[0:1], slab_blocks[2:3]], axis=0)
     stiff = jnp.concatenate([stiff_rows[0], stiff_iface[0]], axis=0)
-    qmat = jnp.einsum("kfg,kgm->kfm", stiff, blocks, preferred_element_type=jnp.float32).astype(
-        jnp.bfloat16
-    )
-    contrib = jnp.einsum("fc,kfm->kcm", prolong[0], qmat, preferred_element_type=jnp.float32)
-    low_agg = slab_aggs[0]
-    up_agg = slab_aggs[2]
-    targets = jnp.concatenate([column_aggs, low_agg[None], up_agg[None]])
+    qmat = jnp.einsum("kfg,kgm->kfm", stiff, blocks, preferred_element_type=F32).astype(BF16)
+    contrib = jnp.einsum("fc,kfm->kcm", prolong[0], qmat, preferred_element_type=F32)
+    targets = jnp.concatenate([column_aggs, slab_aggs[0][None], slab_aggs[2][None]])
     weights = jnp.concatenate(
         [
-            (jnp.arange(SLOTS, dtype=jnp.int32) < live_count[0]).astype(jnp.float32),
-            (group_at > 0).astype(jnp.float32)[None],
-            (group_at < grp_count - 1).astype(jnp.float32)[None],
+            (jnp.arange(SLOTS, dtype=jnp.int32) < live_count[0]).astype(F32),
+            (group_at > 0).astype(F32)[None],
+            (group_at < grp_count - 1).astype(F32)[None],
         ]
     )
     sides = jnp.concatenate([jnp.ones((SLOTS,), jnp.int32), jnp.array([0, 2], jnp.int32)])
-    side_hot = (sides[:, None] == jnp.arange(3, dtype=jnp.int32)[None, :]).astype(jnp.float32)
-    block_hot = (targets[:, None] == jnp.arange(COARSE, dtype=jnp.int32)[None, :]).astype(
-        jnp.float32
-    )
+    side_hot = (sides[:, None] == jnp.arange(3, dtype=jnp.int32)[None, :]).astype(F32)
+    block_hot = (targets[:, None] == jnp.arange(COARSE, dtype=jnp.int32)[None, :]).astype(F32)
     placing = side_hot[:, :, None] * block_hot[:, None, :] * weights[:, None, None]
     partial_value = jnp.einsum("ksb,kcm->csbm", placing, contrib).reshape(NB, 3 * COARSE * NB)
-    partial_value = partial_value.astype(jnp.bfloat16).astype(jnp.float32)
-    own_hot = (jnp.arange(COARSE, dtype=jnp.int32) == aggregate[0]).astype(jnp.float32)
+    partial_value = partial_value.astype(BF16).astype(F32)
+    own_hot = (jnp.arange(COARSE, dtype=jnp.int32) == aggregate[0]).astype(F32)
     spread = (own_hot[:, None, None] * partial_value[None]).reshape(COARSE * NB, 3 * COARSE * NB)
     return lax.psum_scatter(
-        spread.astype(jnp.bfloat16), "dev", scatter_dimension=0, tiled=True
-    ).astype(jnp.float32)
+        spread.astype(BF16), "dev", scatter_dimension=0, tiled=True
+    ).astype(F32)
+
+
+def dot(a, b):
+    return jnp.dot(a, b, preferred_element_type=F32)
+
+
+def left_kernel(rows, iface, own, left, left_iface):
+    turned = own[:NB].T
+    for s in range(2):
+        left_iface[s] = dot(turned, iface[0, s]).astype(BF16)
+    for k in range(SLOTS):
+        left[k] = dot(turned, rows[0, k]).astype(BF16)
+
+
+def iface_kernel(left_iface, below, above, own, here, away, held):
+    core = lax.axis_index("dev") % 2
+    for s, block in enumerate((below, above)):
+        held[s] = dot(left_iface[s], block[:NB]).astype(BF16)
+    for x in range(2):
+        for s in range(2):
+            for c, out in ((core, here), (1 - core, away)):
+                start = pl.multiple_of((2 * x + c) * QUARTER, QUARTER)
+                out[(2 * x + s) * QUARTER : (2 * x + s + 1) * QUARTER] = held[s, pl.ds(start, QUARTER)]
+    row = lax.broadcasted_iota(jnp.int32, (META, NB), 0)
+    marks = jnp.zeros((META, NB), F32)
+    for n, block in enumerate((below, above, own)):
+        marks = jnp.where(row == n, block[NB:].astype(F32), marks)
+    for out in (here, away):
+        out[4 * QUARTER :] = marks.astype(BF16)
+
+
+def row_marks(block, n):
+    return block[4 * QUARTER + n : 4 * QUARTER + n + 1].astype(F32)
+
+
+def pack_kernel(here, got, ours, there, kept, sent):
+    place = lax.axis_index("dev")
+    column, line = (place // 2) % 2, (place // 4).astype(F32)
+    for x, out in ((column, ours), (1 - column, there)):
+        start = pl.multiple_of(2 * x * QUARTER, QUARTER)
+        for r, source in enumerate((here, got)):
+            out[r * QUARTER : (r + 1) * QUARTER] = source[pl.ds(start, QUARTER)]
+        row = lax.broadcasted_iota(jnp.int32, (META, NB), 0)
+        marks = jnp.zeros((META, NB), F32)
+        for r, source in enumerate((here, got)):
+            for n, m in ((r, 0), (2 + r, 2)):
+                marks = jnp.where(row == n, row_marks(source, m), marks)
+        out[HALF:] = marks.astype(BF16)
+    for a, out in ((line, kept), (1.0 - line, sent)):
+        for b in range(COARSE):
+            weights = []
+            for source in (here, got):
+                mark, into = row_marks(source, 2), row_marks(source, 1)
+                weights.append((mark * a + (1.0 - mark) * (1.0 - a)) * (into if b else 1.0 - into))
+            for x in range(2):
+                at = (2 * x + 1) * QUARTER
+                parts = [source[at : at + QUARTER].astype(F32) * w for source, w in zip((here, got), weights)]
+                out[x * QUARTER : (x + 1) * QUARTER, b * NB : (b + 1) * NB] = (parts[0] + parts[1]).astype(out.dtype)
+
+
+def below_sum_kernel(ours, theirs, kept, sent):
+    line = (lax.axis_index("dev") // 4).astype(F32)
+    marks = [v[HALF:].astype(F32) for v in (ours, theirs)]
+    for a, out in ((line, kept), (1.0 - line, sent)):
+        for b in range(COARSE):
+            total = None
+            for v, mark in zip((ours, theirs), marks):
+                for r in range(2):
+                    row_mark, into = mark[2 + r : 3 + r], mark[r : r + 1]
+                    weight = (row_mark * a + (1.0 - row_mark) * (1.0 - a)) * (into if b else 1.0 - into)
+                    value = v[r * QUARTER : (r + 1) * QUARTER].astype(F32) * weight
+                    total = value if total is None else total + value
+            out[:, b * NB : (b + 1) * NB] = total.astype(out.dtype)
+
+
+def above_sum_kernel(ours, got, kept, sent):
+    column = (lax.axis_index("dev") // 2) % 2
+    for x, out in ((column, kept), (1 - column, sent)):
+        at = pl.ds(pl.multiple_of(x * QUARTER, QUARTER), QUARTER)
+        out[...] = (ours[at] + got[at].astype(F32)).astype(out.dtype)
+
+
+def slab_kernel(columns, live, left, b0, b1, b2, b3, b5, b6, b7, kept, sent, held):
+    place = lax.axis_index("dev")
+    core = place % 2
+    held[...] = jnp.zeros_like(held)
+    for t, block in zip(TURNS, (b0, b1, b2, b3, b5, b6, b7)):
+        slot = jnp.int32(SLOTS)
+        for k in range(SLOTS):
+            slot = jnp.where((columns[0, k] ^ place) == t, k, slot)
+
+        @pl.when(slot < live[0])
+        def _():
+            value = dot(left[slot], block[:NB])
+            upper = block[NB : NB + 1].astype(F32)
+            held[0] += value * (1.0 - upper)
+            held[1] += value * upper
+
+    for c, out in ((core, kept), (1 - core, sent)):
+        for x in range(2):
+            start = pl.multiple_of((2 * x + c) * QUARTER, QUARTER)
+            for b in range(COARSE):
+                value = held[b, pl.ds(start, QUARTER)]
+                out[x * QUARTER : (x + 1) * QUARTER, b * NB : (b + 1) * NB] = value.astype(out.dtype)
+
+
+def slab_sum_kernel(ours, got, b0, b1, kept, s2, s4, s6):
+    place = lax.axis_index("dev")
+    column, line = (place // 2) % 2, place // 4
+    side = line.astype(F32)
+    for a, outs in ((side, (kept, s2)), (1.0 - side, (s4, s6))):
+        weights = []
+        for block in (b0, b1):
+            mark = block[NB : NB + 1].astype(F32)
+            mark = jnp.concatenate([mark, mark], axis=1)
+            weights.append(mark * a + (1.0 - mark) * (1.0 - a))
+        for x, out in zip((column, 1 - column), outs):
+            at = pl.ds(pl.multiple_of(x * QUARTER, QUARTER), QUARTER)
+            out[...] = (ours[at] * weights[0] + got[at].astype(F32) * weights[1]).astype(out.dtype)
+
+
+def last_kernel(below, got_below, kept, r2, r4, r6, above, got_above, out):
+    wide = COARSE * NB
+    out[:, :wide] = below[...] + got_below[...].astype(F32)
+    out[:, wide : 2 * wide] = kept[...] + r2[...].astype(F32) + r4[...].astype(F32) + r6[...].astype(F32)
+    out[:, 2 * wide :] = above[...] + got_above[...].astype(F32)
+
+
+def whole():
+    return pl.BlockSpec(memory_space=pltpu.VMEM)
+
+
+def scalars():
+    return pl.BlockSpec(memory_space=pltpu.SMEM)
+
+
+def call(kernel, name, outs, in_specs, scratch=(), limit=16):
+    return pl.pallas_call(
+        kernel,
+        out_shape=tuple(jax.ShapeDtypeStruct(shape, kind) for shape, kind in outs),
+        in_specs=in_specs,
+        out_specs=(whole(),) * len(outs),
+        scratch_shapes=scratch,
+        compiler_params=pltpu.CompilerParams(vmem_limit_bytes=limit * 2**20),
+        name=name,
+    )
+
+
+def after(value, *others):
+    return lax.optimization_barrier((value, *others))[0]
+
+
+def on_square(stiff_rows, stiff_iface, columns, live_count, aggregate, prolong):
+    groups = lax.axis_size("grp")
+    up = [(i, i + 1) for i in range(groups - 1)]
+    down = [(j, i) for i, j in up]
+
+    def hop(block, turn):
+        return lax.ppermute(block, "dev", [(i, i ^ turn) for i in range(8)])
+
+    block_row = lax.broadcasted_iota(jnp.int32, (NB + META, NB), 0) < NB
+    longer = jnp.pad(prolong[0], ((0, META), (0, 0)))
+    own = jnp.where(block_row, longer, aggregate.astype(BF16)[:, None])
+    b5 = hop(own, 5)
+    b2 = hop(own, 2)
+    below = lax.ppermute(own, "grp", up)
+    above = lax.ppermute(own, "grp", down)
+    b7 = hop(b5, 2)
+
+    columns, live_count = after((columns, live_count), b2)
+    left, left_iface = call(left_kernel, "left", (((SLOTS, NB, NB), BF16), ((2, NB, NB), BF16)), [whole()] * 3)(
+        stiff_rows, stiff_iface, after(own, b2, b5)
+    )
+    row = ((4 * QUARTER + META, NB), BF16)
+    here, away = call(iface_kernel, "iface", (row, row), [whole()] * 4, [pltpu.VMEM((2, NB, NB), BF16)])(
+        left_iface, below, above, own
+    )
+    got_here = hop(away, 1)
+    b1 = hop(after(own, here), 1)
+    b3 = hop(after(b2, here), 1)
+    b6 = hop(after(b7, here), 1)
+
+    wide = COARSE * NB
+    packed = (HALF + META, NB)
+    ours, there, line_kept, line_sent = call(
+        pack_kernel, "pack", ((packed, BF16), (packed, BF16), ((HALF, wide), F32), ((HALF, wide), BF16)), [whole()] * 2
+    )(here, got_here)
+    got_line = hop(line_sent, 4)
+    theirs = hop(there, 2)
+
+    kept, sent = call(
+        slab_kernel,
+        "slab",
+        (((HALF, wide), F32), ((HALF, wide), BF16)),
+        [scalars(), scalars()] + [whole()] * 8,
+        [pltpu.VMEM((COARSE, NB, NB), F32)],
+    )(columns, live_count, left, own, b1, b2, b3, b5, b6, b7)
+    got_slab = hop(sent, 1)
+    part = (QUARTER, wide)
+    kept, s2, s4, s6 = call(
+        slab_sum_kernel, "slab_sum", ((part, F32), (part, BF16), (part, BF16), (part, BF16)), [whole()] * 4
+    )(kept, got_slab, own, b1)
+    r2, r4, r6 = hop(s2, 2), hop(s4, 4), hop(s6, 6)
+
+    pair = ((part, F32), (part, BF16))
+    below_kept, below_sent = call(below_sum_kernel, "below_sum", pair, [whole()] * 2)(ours, after(theirs, s2, s4, s6))
+    got_below = hop(below_sent, 4)
+    above_kept, above_sent = call(above_sum_kernel, "above_sum", pair, [whole()] * 2)(line_kept, after(got_line, s2, s4, s6))
+    got_above = hop(above_sent, 2)
+    return call(last_kernel, "last", (((QUARTER, 3 * wide), F32),), [whole()] * 8)(
+        below_kept, got_below, kept, r2, r4, r6, above_kept, got_above
+    )[0]
 
 
 def solution(mesh):
@@ -94,6 +308,7 @@
         P(("grp", "dev"), None, None),
     )
     out_specs = P(("grp", "dev"), None)
+    on_device = on_square if mesh.shape["dev"] == 8 else on_any_slab
     return jax.shard_map(
         on_device, mesh=mesh, in_specs=in_specs, out_specs=out_specs, check_vma=False
     )

time: 136 us -> 46.4 us (0.34)
  waiting for transfers between devices: 54.3 us -> 12.3 us
  local copies, waits for them, and re-layouts: 25.3 us -> 2.55 us
  between operations: 14.8 us -> 1.44 us
  matrix products: 9.81 us -> 0 us
  other arithmetic: 7.85 us -> 1.09 us
  Pallas kernels: 0 us -> 6.6 us
  starting transfers between devices: 23.8 us -> 22.3 us
    reduce_scatter x1 -> x0, waiting for transfers between devices: 46.1 us -> none  [on_device(): lax.psum_scatter(spread.astype(jnp.bfloat16), 'dev', scatter_dimension=0,...]
    dot_general x2 -> x0, matrix products: 9.81 us -> none  [the longest x1 6.32 us: on_device(): jnp.einsum('fc,kfm->kcm', prolong[0], qmat, preferred_element_type=jnp.fl...]
    convert_element_type x2 -> x0, local copies, waits for them, and re-layouts: 9.53 us -> none  [on_device(): partial_value = partial_value.astype(jnp.bfloat16).astype(jnp.float32)]
    pallas_call x0 -> x8, Pallas kernels: none -> 6.6 us  [the longest x1 2.51 us: on_square(): call(slab_kernel, 'slab', (((HALF, wide), F32), ((HALF, wide), BF16)), [s...]
    convert_element_type x5 -> x0, other arithmetic: 4.76 us -> none  [the longest x1 2.2 us: on_device(): spread.astype(jnp.bfloat16)]
    concatenate x3 -> x0, local copies, waits for them, and re-layouts: 4.74 us -> none  [the longest x1 3.89 us: on_device(): window_aggs = jnp.concatenate(agg_list, axis=0)]
    ppermute x16 -> x17, waiting for transfers between devices: 8.13 us -> 12.3 us  [the longest x15 12.3 us: hop(): return lax.ppermute(block, 'dev', [(i, i ^ turn) for i in range(8)])]
    dot_general x1 -> x0, local copies, waits for them, and re-layouts: 3.31 us -> none  [on_device(): jnp.einsum('fc,kfm->kcm', prolong[0], qmat, preferred_element_type=jnp.fl...]
  transfers between devices with their start and end apart: 17 -> 17, of which waited for: 3 -> 7; matrix products, arithmetic and copies ran while one was open for 12% -> 0% of each run, Pallas kernels for 0% -> 12%
where the time goes in v2:
time: 46.4 us; the launch traced here: 46.3 us
  starting transfers between devices  22.3 us (48%)
  waiting for transfers between devices  12.3 us (27%)
  Pallas kernels  6.6 us (14%)
  local copies, waits for them, and re-layouts  2.55 us (5%)
  between operations  1.44 us (3%)
  other arithmetic  1.09 us (2%)
    ppermute x15, starting transfers between devices, hop(): return lax.ppermute(block, 'dev', [(i, i ^ turn) for i in range(8)])  16.5 us
    ppermute x15, waiting for transfers between devices, hop(): return lax.ppermute(block, 'dev', [(i, i ^ turn) for i in range(8)])  12.3 us
    ppermute x1, starting transfers between devices, on_square(): below = lax.ppermute(own, 'grp', up)  4.57 us
    unnamed x6, local copies, waits for them, and re-layouts  2.55 us
    pallas_call x1, Pallas kernels, on_square(): call(slab_kernel, 'slab', (((HALF, wide), F32), ((HALF, wide), BF16)), [s...  2.51 us
    pallas_call x1, Pallas kernels, on_square(): call(left_kernel, 'left', (((SLOTS, NB, NB), BF16), ((2, NB, NB), BF16)),...  1.63 us
    ppermute x1, starting transfers between devices, on_square(): above = lax.ppermute(own, 'grp', down)  1.28 us
    select_n x1, other arithmetic, on_square(): own = jnp.where(block_row, longer, aggregate.astype(BF16)[:, None])  1.09 us
  transfers between devices with their start and end apart: 17, of which 7 were waited for; matrix products, arithmetic and copies ran while one was open for 0% of the time, Pallas kernels for 12%

profile of v2, /device:TPU:0, one launch (start us, length us, event | category | flops | bytes accessed | tf_op | source)
XLA Modules:
  0.0 46.3 jit_solution(15525759633127072569)
XLA Ops:
  0.7 1.1 %pad_select_fusion.own.b0 = bf16[400,384]{1,0:T(8,128)(2,1)S(1)} fusion(bf16[384,384]{1,0:T(8,128)(2,1)} %bitcast.2, pred[400]{0:T(512)(128)(4,1)S(1)} %iota_compare_fusion, bf16[]{:T(256)} %bitcast.1), kind=kLoop, calls=%fused_computation | loop fusion | flops 153600 | bytes 602514 | tf_op jit(solution)/shard_map/jit(_where)/select_n | solution.py:249
  1.8 2.5 %collective-permute-start.1 = (bf16[400,384]{1,0:T(8,128)(2,1)S(1)}, bf16[400,384]{1,0:T(8,128)(2,1)S(1)}, u32[]{:S(2)}, u32[]{:S(2)}) collective-permute-start(bf16[400,384]{1,0:T(8,128)(2,1)S(1)} %pad_select_fusion.own.b0), channel_id=1, source_target_pairs={{0,5},{1,4},{2,7},{3,6},{4,1},{5,0},{6,3},{7,2},{8,13},{9,12},{10,... | collective-permute-start | bytes 921608 | tf_op jit(solution)/shard_map/ppermute | solution.py:245
  4.2 1.5 %collective-permute-start = (bf16[400,384]{1,0:T(8,128)(2,1)S(1)}, bf16[400,384]{1,0:T(8,128)(2,1)S(1)}, u32[]{:S(2)}, u32[]{:S(2)}) collective-permute-start(bf16[400,384]{1,0:T(8,128)(2,1)S(1)} %pad_select_fusion.own.b0), channel_id=1, source_target_pairs={{0,2},{1,3},{2,0},{3,1},{4,6},{5,7},{6,4},{7,5},{8,10},{9,11},{10,... | collective-permute-start | bytes 921608 | tf_op jit(solution)/shard_map/ppermute | solution.py:245
  5.7 1.3 %collective-permute-start.3 = (bf16[400,384]{1,0:T(8,128)(2,1)S(1)}, bf16[400,384]{1,0:T(8,128)(2,1)S(1)}, u32[]{:S(2)}, u32[]{:S(2)}) collective-permute-start(bf16[400,384]{1,0:T(8,128)(2,1)S(1)} %pad_select_fusion.own.b0), channel_id=1, source_target_pairs={{8,0},{16,8},{24,16},{9,1},{17,9},{25,17},{10,2},{18,10},{26,18},{... | collective-permute-start | bytes 921608 | tf_op jit(solution)/shard_map/ppermute | solution.py:253
  7.0 4.6 %collective-permute-start.2 = (bf16[400,384]{1,0:T(8,128)(2,1)S(1)}, bf16[400,384]{1,0:T(8,128)(2,1)S(1)}, u32[]{:S(2)}, u32[]{:S(2)}) collective-permute-start(bf16[400,384]{1,0:T(8,128)(2,1)S(1)} %pad_select_fusion.own.b0), channel_id=1, source_target_pairs={{0,8},{8,16},{16,24},{1,9},{9,17},{17,25},{2,10},{10,18},{18,26},{... | collective-permute-start | bytes 921608 | tf_op jit(solution)/shard_map/ppermute | solution.py:252
  11.9 2.4 %collective-permute-start.8 = (bf16[400,384]{1,0:T(8,128)(2,1)S(1)}, bf16[400,384]{1,0:T(8,128)(2,1)S(1)}, u32[]{:S(2)}, u32[]{:S(2)}) collective-permute-start(bf16[400,384]{1,0:T(8,128)(2,1)S(1)} %collective-permute-done.1.b5), channel_id=1, source_target_pairs={{0,2},{1,3},{2,0},{3,1},{4,6},{5,7},{6,4},{7,5},{8,10},{9,11},{10,... | collective-permute-start | bytes 921608 | tf_op jit(solution)/shard_map/ppermute | solution.py:245
  14.3 1.5 %copy-done = bf16[1,6,384,384]{3,2,1,0:T(8,128)(2,1)S(1)} copy-done((bf16[1,6,384,384]{3,2,1,0:T(8,128)(2,1)S(1)}, bf16[1,6,384,384]{3,2,1,0:T(8,128)(2,1)}, u32[]{:S(2)}) %copy-start) | copy-done | bytes 1769496
  15.8 1.1 %copy-done.1 = bf16[1,2,384,384]{3,2,1,0:T(8,128)(2,1)S(1)} copy-done((bf16[1,2,384,384]{3,2,1,0:T(8,128)(2,1)S(1)}, bf16[1,2,384,384]{3,2,1,0:T(8,128)(2,1)}, u32[]{:S(2)}) %copy-start.1) | copy-done | bytes 589848
  16.8 1.6 %left.1 = (bf16[6,384,384]{2,1,0:T(8,128)(2,1)S(1)}, bf16[2,384,384]{2,1,0:T(8,128)(2,1)S(1)}) custom-call(bf16[1,6,384,384]{3,2,1,0:T(8,128)(2,1)S(1)} %copy-done, bf16[1,2,384,384]{3,2,1,0:T(8,128)(2,1)S(1)} %copy-done.1, bf16[400,384]{1,0:T(8,128)(2,1)S(1)} %pad_select_fusion.own.b0), custom_call_target="tpu_custom_call" | custom-call | tf_op jit(solution)/shard_map/left/pallas_call | solution.py:257
  18.5 0.6 %iface.3 = (bf16[400,384]{1,0:T(8,128)(2,1)S(1)}, bf16[400,384]{1,0:T(8,128)(2,1)S(1)}) custom-call(bf16[2,384,384]{2,1,0:T(8,128)(2,1)S(1)} %get-tuple-element.32.left_iface, bf16[400,384]{1,0:T(8,128)(2,1)S(1)} %collective-permute-done.2.below, bf16[400,384]{1,0:T(8,128)(2,1)S(1)} %collective-permute-done.3.above, bf16[400,384]{1,0:T(8,128)(2,1)S(1)} %pad_select_fusion.own.b0), custom_call_target="tpu_custom_call" | custom-call | tf_op jit(solution)/shard_map/iface/pallas_call | solution.py:261
  19.7 2.2 %collective-permute-done.8.b7 = bf16[400,384]{1,0:T(8,128)(2,1)S(1)} collective-permute-done((bf16[400,384]{1,0:T(8,128)(2,1)S(1)}, bf16[400,384]{1,0:T(8,128)(2,1)S(1)}, u32[]{:S(2)}, u32[]{:S(2)}) %collective-permute-start.8) | collective-permute-done | bytes 307232 | tf_op jit(solution)/shard_map/ppermute | solution.py:245
  21.9 0.5 %collective-permute-start.4 = (bf16[400,384]{1,0:T(8,128)(2,1)S(1)}, bf16[400,384]{1,0:T(8,128)(2,1)S(1)}, u32[]{:S(2)}, u32[]{:S(2)}) collective-permute-start(bf16[400,384]{1,0:T(8,128)(2,1)S(1)} %get-tuple-element.34), channel_id=1, source_target_pairs={{0,1},{1,0},{2,3},{3,2},{4,5},{5,4},{6,7},{7,6},{8,9},{9,8},{10,11... | collective-permute-start | bytes 921608 | tf_op jit(solution)/shard_map/ppermute | solution.py:245
  23.5 2.5 %slab.1 = (f32[192,768]{1,0:T(8,128)S(1)}, bf16[192,768]{1,0:T(8,128)(2,1)S(1)}) custom-call(s32[1,6]{1,0:T(1,128)S(1)} %copy-done.2, s32[1]{0:T(128)S(6)} %copy.7.live, bf16[6,384,384]{2,1,0:T(8,128)(2,1)S(1)} %get-tuple-element.39.left, bf16[400,384]{1,0:T(8,128)(2,1)S(1)} %pad_select_fusion.own.b0, bf16[400,384]{1,0:T(8,128)(2,1)S(1)} %collective-permute-done.6.b1, ...), custom_call_target="tpu_custom_call" | custom-call | tf_op jit(solution)/shard_map/slab/pallas_call | solution.py:277
  26.0 0.6 %collective-permute-start.10 = (bf16[192,768]{1,0:T(8,128)(2,1)S(1)}, bf16[192,768]{1,0:T(8,128)(2,1)S(1)}, u32[]{:S(2)}, u32[]{:S(2)}) collective-permute-start(bf16[192,768]{1,0:T(8,128)(2,1)S(1)} %get-tuple-element.44), channel_id=1, source_target_pairs={{0,1},{1,0},{2,3},{3,2},{4,5},{5,4},{6,7},{7,6},{8,9},{9,8},{10,11... | collective-permute-start | bytes 884744 | tf_op jit(solution)/shard_map/ppermute | solution.py:245
  27.3 2.5 %collective-permute-start.5 = (bf16[208,384]{1,0:T(8,128)(2,1)S(1)}, bf16[208,384]{1,0:T(8,128)(2,1)S(1)}, u32[]{:S(2)}, u32[]{:S(2)}) collective-permute-start(bf16[208,384]{1,0:T(8,128)(2,1)S(1)} %get-tuple-element.36), channel_id=1, source_target_pairs={{0,2},{1,3},{2,0},{3,1},{4,6},{5,7},{6,4},{7,5},{8,10},{9,11},{10,... | collective-permute-start | bytes 479240 | tf_op jit(solution)/shard_map/ppermute | solution.py:245
  30.1 1.1 %collective-permute-start.13 = (bf16[96,768]{1,0:T(8,128)(2,1)S(1)}, bf16[96,768]{1,0:T(8,128)(2,1)S(1)}, u32[]{:S(2)}, u32[]{:S(2)}) collective-permute-start(bf16[96,768]{1,0:T(8,128)(2,1)S(1)} %get-tuple-element.46), channel_id=1, source_target_pairs={{0,4},{1,5},{2,6},{3,7},{4,0},{5,1},{6,2},{7,3},{8,12},{9,13},{10,... | collective-permute-start | bytes 442376 | tf_op jit(solution)/shard_map/ppermute | solution.py:245
  31.2 2.4 %collective-permute-start.14 = (bf16[96,768]{1,0:T(8,128)(2,1)S(1)}, bf16[96,768]{1,0:T(8,128)(2,1)S(1)}, u32[]{:S(2)}, u32[]{:S(2)}) collective-permute-start(bf16[96,768]{1,0:T(8,128)(2,1)S(1)} %get-tuple-element.47), channel_id=1, source_target_pairs={{0,6},{1,7},{2,4},{3,5},{4,2},{5,3},{6,0},{7,1},{8,14},{9,15},{10,... | collective-permute-start | bytes 442376 | tf_op jit(solution)/shard_map/ppermute | solution.py:245
  33.6 1.1 %collective-permute-done.5.theirs = bf16[208,384]{1,0:T(8,128)(2,1)S(1)} collective-permute-done((bf16[208,384]{1,0:T(8,128)(2,1)S(1)}, bf16[208,384]{1,0:T(8,128)(2,1)S(1)}, u32[]{:S(2)}, u32[]{:S(2)}) %collective-permute-start.5) | collective-permute-done | bytes 159776 | tf_op jit(solution)/shard_map/ppermute | solution.py:245
  35.0 1.3 %collective-permute-start.11 = (bf16[96,768]{1,0:T(8,128)(2,1)S(1)}, bf16[96,768]{1,0:T(8,128)(2,1)S(1)}, u32[]{:S(2)}, u32[]{:S(2)}) collective-permute-start(bf16[96,768]{1,0:T(8,128)(2,1)S(1)} %get-tuple-element.50), channel_id=1, source_target_pairs={{0,4},{1,5},{2,6},{3,7},{4,0},{5,1},{6,2},{7,3},{8,12},{9,13},{10,... | collective-permute-start | bytes 442376 | tf_op jit(solution)/shard_map/ppermute | solution.py:245
  36.3 1.2 %collective-permute-done.15.got = bf16[192,768]{1,0:T(8,128)(2,1)S(1)} collective-permute-done((bf16[192,768]{1,0:T(8,128)(2,1)S(1)}, bf16[192,768]{1,0:T(8,128)(2,1)S(1)}, u32[]{:S(2)}, u32[]{:S(2)}) %collective-permute-start.15) | collective-permute-done | bytes 294944 | tf_op jit(solution)/shard_map/ppermute | solution.py:245
  37.6 0.7 %collective-permute-start.16 = (bf16[96,768]{1,0:T(8,128)(2,1)S(1)}, bf16[96,768]{1,0:T(8,128)(2,1)S(1)}, u32[]{:S(2)}, u32[]{:S(2)}) collective-permute-start(bf16[96,768]{1,0:T(8,128)(2,1)S(1)} %get-tuple-element.56), channel_id=1, source_target_pairs={{0,2},{1,3},{2,0},{3,1},{4,6},{5,7},{6,4},{7,5},{8,10},{9,11},{10,... | collective-permute-start | bytes 442376 | tf_op jit(solution)/shard_map/ppermute | solution.py:245
  38.3 4.8 %collective-permute-done.13.r4 = bf16[96,768]{1,0:T(8,128)(2,1)S(1)} collective-permute-done((bf16[96,768]{1,0:T(8,128)(2,1)S(1)}, bf16[96,768]{1,0:T(8,128)(2,1)S(1)}, u32[]{:S(2)}, u32[]{:S(2)}) %collective-permute-start.13) | collective-permute-done | bytes 147488 | tf_op jit(solution)/shard_map/ppermute | solution.py:245
  43.1 2.2 %collective-permute-done.11.got_below = bf16[96,768]{1,0:T(8,128)(2,1)S(1)} collective-permute-done((bf16[96,768]{1,0:T(8,128)(2,1)S(1)}, bf16[96,768]{1,0:T(8,128)(2,1)S(1)}, u32[]{:S(2)}, u32[]{:S(2)}) %collective-permute-start.11) | collective-permute-done | bytes 147488 | tf_op jit(solution)/shard_map/ppermute | solution.py:245
  45.3 1.0 %last.1 = f32[96,2304]{1,0:T(8,128)} custom-call(f32[96,768]{1,0:T(8,128)S(1)} %get-tuple-element.49.below, bf16[96,768]{1,0:T(8,128)(2,1)S(1)} %collective-permute-done.11.got_below, f32[96,768]{1,0:T(8,128)S(1)} %get-tuple-element.51.kept, bf16[96,768]{1,0:T(8,128)(2,1)S(1)} %collective-permute-done.12.r2, bf16[96,768]{1,0:T(8,128)(2,1)S(1)} %collective-permute-done.13.r4, ...), custom_call_target="tpu_custom_call" | custom-call | tf_op jit(solution)/shard_map/last/pallas_call | solution.py:296
  (26 shorter events, 2.7 us)
Async XLA Ops:
  0.7 22.8 %copy-start.2 = (s32[1,6]{1,0:T(1,128)S(1)}, s32[1,6]{1,0:T(1,128)}, u32[]{:S(2)}) copy-start(s32[1,6]{1,0:T(1,128)} %columns) | copy-start | bytes 76
  1.8 10.1 %collective-permute-start.1 = (bf16[400,384]{1,0:T(8,128)(2,1)S(1)}, bf16[400,384]{1,0:T(8,128)(2,1)S(1)}, u32[]{:S(2)}, u32[]{:S(2)}) collective-permute-start(bf16[400,384]{1,0:T(8,128)(2,1)S(1)} %pad_select_fusion.own.b0), channel_id=1, source_target_pairs={{0,5},{1,4},{2,7},{3,6},{4,1},{5,0},{6,3},{7,2},{8,13},{9,12},{10,... | collective-permute-start | bytes 921608 | tf_op jit(solution)/shard_map/ppermute | solution.py:245
  4.2 10.0 %collective-permute-start = (bf16[400,384]{1,0:T(8,128)(2,1)S(1)}, bf16[400,384]{1,0:T(8,128)(2,1)S(1)}, u32[]{:S(2)}, u32[]{:S(2)}) collective-permute-start(bf16[400,384]{1,0:T(8,128)(2,1)S(1)} %pad_select_fusion.own.b0), channel_id=1, source_target_pairs={{0,2},{1,3},{2,0},{3,1},{4,6},{5,7},{6,4},{7,5},{8,10},{9,11},{10,... | collective-permute-start | bytes 921608 | tf_op jit(solution)/shard_map/ppermute | solution.py:245
  5.7 12.7 %collective-permute-start.3 = (bf16[400,384]{1,0:T(8,128)(2,1)S(1)}, bf16[400,384]{1,0:T(8,128)(2,1)S(1)}, u32[]{:S(2)}, u32[]{:S(2)}) collective-permute-start(bf16[400,384]{1,0:T(8,128)(2,1)S(1)} %pad_select_fusion.own.b0), channel_id=1, source_target_pairs={{8,0},{16,8},{24,16},{9,1},{17,9},{25,17},{10,2},{18,10},{26,18},{... | collective-permute-start | bytes 921608 | tf_op jit(solution)/shard_map/ppermute | solution.py:253
  7.0 11.4 %collective-permute-start.2 = (bf16[400,384]{1,0:T(8,128)(2,1)S(1)}, bf16[400,384]{1,0:T(8,128)(2,1)S(1)}, u32[]{:S(2)}, u32[]{:S(2)}) collective-permute-start(bf16[400,384]{1,0:T(8,128)(2,1)S(1)} %pad_select_fusion.own.b0), channel_id=1, source_target_pairs={{0,8},{8,16},{16,24},{1,9},{9,17},{17,25},{2,10},{10,18},{18,26},{... | collective-permute-start | bytes 921608 | tf_op jit(solution)/shard_map/ppermute | solution.py:252
  11.9 10.0 %collective-permute-start.8 = (bf16[400,384]{1,0:T(8,128)(2,1)S(1)}, bf16[400,384]{1,0:T(8,128)(2,1)S(1)}, u32[]{:S(2)}, u32[]{:S(2)}) collective-permute-start(bf16[400,384]{1,0:T(8,128)(2,1)S(1)} %collective-permute-done.1.b5), channel_id=1, source_target_pairs={{0,2},{1,3},{2,0},{3,1},{4,6},{5,7},{6,4},{7,5},{8,10},{9,11},{10,... | collective-permute-start | bytes 921608 | tf_op jit(solution)/shard_map/ppermute | solution.py:245
  14.3 1.5 %copy-start = (bf16[1,6,384,384]{3,2,1,0:T(8,128)(2,1)S(1)}, bf16[1,6,384,384]{3,2,1,0:T(8,128)(2,1)}, u32[]{:S(2)}) copy-start(bf16[1,6,384,384]{3,2,1,0:T(8,128)(2,1)} %rows.1) | copy-start | bytes 5308420
  15.8 1.1 %copy-start.1 = (bf16[1,2,384,384]{3,2,1,0:T(8,128)(2,1)S(1)}, bf16[1,2,384,384]{3,2,1,0:T(8,128)(2,1)}, u32[]{:S(2)}) copy-start(bf16[1,2,384,384]{3,2,1,0:T(8,128)(2,1)} %iface.2) | copy-start | bytes 1769476
  19.1 3.9 %collective-permute-start.6 = (bf16[400,384]{1,0:T(8,128)(2,1)S(1)}, bf16[400,384]{1,0:T(8,128)(2,1)S(1)}, u32[]{:S(2)}, u32[]{:S(2)}) collective-permute-start(bf16[400,384]{1,0:T(8,128)(2,1)S(1)} %pad_select_fusion.own.b0), channel_id=1, source_target_pairs={{0,1},{1,0},{2,3},{3,2},{4,5},{5,4},{6,7},{7,6},{8,9},{9,8},{10,11... | collective-permute-start | bytes 921608 | tf_op jit(solution)/shard_map/ppermute | solution.py:245
  19.2 3.9 %collective-permute-start.7 = (bf16[400,384]{1,0:T(8,128)(2,1)S(1)}, bf16[400,384]{1,0:T(8,128)(2,1)S(1)}, u32[]{:S(2)}, u32[]{:S(2)}) collective-permute-start(bf16[400,384]{1,0:T(8,128)(2,1)S(1)} %collective-permute-done.b2), channel_id=1, source_target_pairs={{0,1},{1,0},{2,3},{3,2},{4,5},{5,4},{6,7},{7,6},{8,9},{9,8},{10,11... | collective-permute-start | bytes 921608 | tf_op jit(solution)/shard_map/ppermute | solution.py:245
  21.9 1.6 %collective-permute-start.9 = (bf16[400,384]{1,0:T(8,128)(2,1)S(1)}, bf16[400,384]{1,0:T(8,128)(2,1)S(1)}, u32[]{:S(2)}, u32[]{:S(2)}) collective-permute-start(bf16[400,384]{1,0:T(8,128)(2,1)S(1)} %collective-permute-done.8.b7), channel_id=1, source_target_pairs={{0,1},{1,0},{2,3},{3,2},{4,5},{5,4},{6,7},{7,6},{8,9},{9,8},{10,11... | collective-permute-start | bytes 921608 | tf_op jit(solution)/shard_map/ppermute | solution.py:245
  21.9 4.7 %collective-permute-start.4 = (bf16[400,384]{1,0:T(8,128)(2,1)S(1)}, bf16[400,384]{1,0:T(8,128)(2,1)S(1)}, u32[]{:S(2)}, u32[]{:S(2)}) collective-permute-start(bf16[400,384]{1,0:T(8,128)(2,1)S(1)} %get-tuple-element.34), channel_id=1, source_target_pairs={{0,1},{1,0},{2,3},{3,2},{4,5},{5,4},{6,7},{7,6},{8,9},{9,8},{10,11... | collective-permute-start | bytes 921608 | tf_op jit(solution)/shard_map/ppermute | solution.py:245
  26.0 3.8 %collective-permute-start.10 = (bf16[192,768]{1,0:T(8,128)(2,1)S(1)}, bf16[192,768]{1,0:T(8,128)(2,1)S(1)}, u32[]{:S(2)}, u32[]{:S(2)}) collective-permute-start(bf16[192,768]{1,0:T(8,128)(2,1)S(1)} %get-tuple-element.44), channel_id=1, source_target_pairs={{0,1},{1,0},{2,3},{3,2},{4,5},{5,4},{6,7},{7,6},{8,9},{9,8},{10,11... | collective-permute-start | bytes 884744 | tf_op jit(solution)/shard_map/ppermute | solution.py:245
  26.8 10.7 %collective-permute-start.15 = (bf16[192,768]{1,0:T(8,128)(2,1)S(1)}, bf16[192,768]{1,0:T(8,128)(2,1)S(1)}, u32[]{:S(2)}, u32[]{:S(2)}) collective-permute-start(bf16[192,768]{1,0:T(8,128)(2,1)S(1)} %get-tuple-element.53), channel_id=1, source_target_pairs={{0,4},{1,5},{2,6},{3,7},{4,0},{5,1},{6,2},{7,3},{8,12},{9,13},{10,... | collective-permute-start | bytes 884744 | tf_op jit(solution)/shard_map/ppermute | solution.py:245
  27.3 7.4 %collective-permute-start.5 = (bf16[208,384]{1,0:T(8,128)(2,1)S(1)}, bf16[208,384]{1,0:T(8,128)(2,1)S(1)}, u32[]{:S(2)}, u32[]{:S(2)}) collective-permute-start(bf16[208,384]{1,0:T(8,128)(2,1)S(1)} %get-tuple-element.36), channel_id=1, source_target_pairs={{0,2},{1,3},{2,0},{3,1},{4,6},{5,7},{6,4},{7,5},{8,10},{9,11},{10,... | collective-permute-start | bytes 479240 | tf_op jit(solution)/shard_map/ppermute | solution.py:245
  30.0 8.2 %collective-permute-start.12 = (bf16[96,768]{1,0:T(8,128)(2,1)S(1)}, bf16[96,768]{1,0:T(8,128)(2,1)S(1)}, u32[]{:S(2)}, u32[]{:S(2)}) collective-permute-start(bf16[96,768]{1,0:T(8,128)(2,1)S(1)} %get-tuple-element.45), channel_id=1, source_target_pairs={{0,2},{1,3},{2,0},{3,1},{4,6},{5,7},{6,4},{7,5},{8,10},{9,11},{10,... | collective-permute-start | bytes 442376 | tf_op jit(solution)/shard_map/ppermute | solution.py:245
  30.1 13.0 %collective-permute-start.13 = (bf16[96,768]{1,0:T(8,128)(2,1)S(1)}, bf16[96,768]{1,0:T(8,128)(2,1)S(1)}, u32[]{:S(2)}, u32[]{:S(2)}) collective-permute-start(bf16[96,768]{1,0:T(8,128)(2,1)S(1)} %get-tuple-element.46), channel_id=1, source_target_pairs={{0,4},{1,5},{2,6},{3,7},{4,0},{5,1},{6,2},{7,3},{8,12},{9,13},{10,... | collective-permute-start | bytes 442376 | tf_op jit(solution)/shard_map/ppermute | solution.py:245
  31.2 11.9 %collective-permute-start.14 = (bf16[96,768]{1,0:T(8,128)(2,1)S(1)}, bf16[96,768]{1,0:T(8,128)(2,1)S(1)}, u32[]{:S(2)}, u32[]{:S(2)}) collective-permute-start(bf16[96,768]{1,0:T(8,128)(2,1)S(1)} %get-tuple-element.47), channel_id=1, source_target_pairs={{0,6},{1,7},{2,4},{3,5},{4,2},{5,3},{6,0},{7,1},{8,14},{9,15},{10,... | collective-permute-start | bytes 442376 | tf_op jit(solution)/shard_map/ppermute | solution.py:245
  35.0 10.3 %collective-permute-start.11 = (bf16[96,768]{1,0:T(8,128)(2,1)S(1)}, bf16[96,768]{1,0:T(8,128)(2,1)S(1)}, u32[]{:S(2)}, u32[]{:S(2)}) collective-permute-start(bf16[96,768]{1,0:T(8,128)(2,1)S(1)} %get-tuple-element.50), channel_id=1, source_target_pairs={{0,4},{1,5},{2,6},{3,7},{4,0},{5,1},{6,2},{7,3},{8,12},{9,13},{10,... | collective-permute-start | bytes 442376 | tf_op jit(solution)/shard_map/ppermute | solution.py:245
  37.6 7.8 %collective-permute-start.16 = (bf16[96,768]{1,0:T(8,128)(2,1)S(1)}, bf16[96,768]{1,0:T(8,128)(2,1)S(1)}, u32[]{:S(2)}, u32[]{:S(2)}) collective-permute-start(bf16[96,768]{1,0:T(8,128)(2,1)S(1)} %get-tuple-element.56), channel_id=1, source_target_pairs={{0,2},{1,3},{2,0},{3,1},{4,6},{5,7},{6,4},{7,5},{8,10},{9,11},{10,... | collective-permute-start | bytes 442376 | tf_op jit(solution)/shard_map/ppermute | solution.py:245

commit v3 on v2

v3 whole, which is shorter than its diff:
```python
import jax
import jax.numpy as jnp
from jax import lax
from jax.experimental import pallas as pl
from jax.experimental.pallas import tpu as pltpu
from jax.sharding import PartitionSpec as P

NB = 384
SLOTS = 6
REACH = 3
COARSE = 2
QUARTER = NB // 4
HALF = NB // 2
META = 16
MARKED = NB + META
TURNS = (0, 1, 2, 3, 5, 6, 7)
WEIGHT = {'own': 4000000000, 'left': 1000000000, 'iface': 4000000000, 'pack': 4000000000, 'slab': 4000000000, 'slab_sum': 4000000000, 'below_sum': 4000000000, 'above_sum': 4000000000, 'last': 4000000000}
F32 = jnp.float32
BF16 = jnp.bfloat16


def passed_along(block, axis, distance):
    devices = range(lax.axis_size(axis))
    route = [((i - distance) % len(devices), i) for i in devices]
    return lax.ppermute(block, axis, route)


def extended(array, sides, width):
    for axis, dim in sides:
        count, length = (lax.axis_size(axis), array.shape[dim])
        up = [(i, (i + 1) % count) for i in range(count - 1)]
        down = [(j, i) for i, j in up]
        last = lax.slice_in_dim(array, length - width, length, axis=dim)
        initial = lax.slice_in_dim(array, 0, width, axis=dim)
        before = lax.ppermute(last, axis, up)
        after = lax.ppermute(initial, axis, down)
        array = jnp.concatenate([before, array, after], axis=dim)
    return array


def on_any_slab(stiff_rows, stiff_iface, columns, live_count, aggregate, prolong):
    dev_count = lax.axis_size("dev")
    grp_count = lax.axis_size("grp")
    group_at = lax.axis_index("grp")
    place_at = lax.axis_index("dev")
    my_columns = columns[0]
    block_list = []
    agg_list = []
    for offset in range(-REACH, REACH + 1):
        if offset == 0:
            block_list.append(prolong)
            agg_list.append(aggregate)
        else:
            got = passed_along((prolong, aggregate), "dev", -offset)
            block_list.append(got[0])
            agg_list.append(got[1])
    window_blocks = jnp.concatenate(block_list, axis=0)
    window_aggs = jnp.concatenate(agg_list, axis=0)
    offsets = (my_columns - place_at + dev_count + REACH) % dev_count
    panels = jnp.take(window_blocks, offsets, axis=0)
    column_aggs = jnp.take(window_aggs, offsets, axis=0)
    slab_blocks, slab_aggs = (
        extended(prolong, (("grp", 0),), 1),
        extended(aggregate, (("grp", 0),), 1),
    )
    blocks = jnp.concatenate([panels, slab_blocks[0:1], slab_blocks[2:3]], axis=0)
    stiff = jnp.concatenate([stiff_rows[0], stiff_iface[0]], axis=0)
    qmat = jnp.einsum("kfg,kgm->kfm", stiff, blocks, preferred_element_type=F32).astype(BF16)
    contrib = jnp.einsum("fc,kfm->kcm", prolong[0], qmat, preferred_element_type=F32)
    targets = jnp.concatenate([column_aggs, slab_aggs[0][None], slab_aggs[2][None]])
    weights = jnp.concatenate(
        [
            (jnp.arange(SLOTS, dtype=jnp.int32) < live_count[0]).astype(F32),
            (group_at > 0).astype(F32)[None],
            (group_at < grp_count - 1).astype(F32)[None],
        ]
    )
    sides = jnp.concatenate([jnp.ones((SLOTS,), jnp.int32), jnp.array([0, 2], jnp.int32)])
    side_hot = (sides[:, None] == jnp.arange(3, dtype=jnp.int32)[None, :]).astype(F32)
    block_hot = (targets[:, None] == jnp.arange(COARSE, dtype=jnp.int32)[None, :]).astype(F32)
    placing = side_hot[:, :, None] * block_hot[:, None, :] * weights[:, None, None]
    partial_value = jnp.einsum("ksb,kcm->csbm", placing, contrib).reshape(NB, 3 * COARSE * NB)
    partial_value = partial_value.astype(BF16).astype(F32)
    own_hot = (jnp.arange(COARSE, dtype=jnp.int32) == aggregate[0]).astype(F32)
    spread = (own_hot[:, None, None] * partial_value[None]).reshape(COARSE * NB, 3 * COARSE * NB)
    return lax.psum_scatter(
        spread.astype(BF16), "dev", scatter_dimension=0, tiled=True
    ).astype(F32)


def dot(a, b):
    return jnp.dot(a, b, preferred_element_type=F32)


def own_kernel(aggregate, prolong, own):
    own[:NB] = prolong[0]
    own[NB:] = jnp.broadcast_to(aggregate[...], (META, NB)).astype(F32).astype(BF16)


def left_kernel(columns, live, rows, iface, own, left, left_iface):
    place = lax.axis_index("dev")
    turned = own[:NB].T
    for s in range(2):
        left_iface[s] = dot(turned, iface[0, s]).astype(BF16)
    left[...] = jnp.zeros_like(left)
    for k in range(SLOTS):

        @pl.when(k < live[0])
        def _():
            left[columns[0, k] ^ place] = dot(turned, rows[0, k]).astype(BF16)


def iface_kernel(left_iface, below, above, own, here0, here1, away0, away1, held):
    core = lax.axis_index("dev") % 2
    row = lax.broadcasted_iota(jnp.int32, (META, NB), 0)
    for s, (block, here, away) in enumerate(((below, here0, away0), (above, here1, away1))):
        held[s] = dot(left_iface[s], block[:NB]).astype(BF16)
        marks = jnp.where(row == 0, block[NB:].astype(F32), own[NB:].astype(F32)).astype(BF16)
        for c, out in ((core, here), (1 - core, away)):
            for x in range(2):
                start = pl.multiple_of((2 * x + c) * QUARTER, QUARTER)
                out[x * QUARTER : (x + 1) * QUARTER] = held[s, pl.ds(start, QUARTER)]
            out[HALF:] = marks


def row_marks(block, n):
    return block[HALF:].astype(F32)[n : n + 1]


def pack_kernel(here0, here1, got0, got1, ours, there, kept, sent):
    place = lax.axis_index("dev")
    column, line = (place // 2) % 2, (place // 4).astype(F32)
    row = lax.broadcasted_iota(jnp.int32, (META, NB), 0)
    marks = jnp.zeros((META, NB), F32)
    for r, source in enumerate((here0, got0)):
        for n, m in ((r, 0), (2 + r, 1)):
            marks = jnp.where(row == n, row_marks(source, m), marks)
    for x, out in ((column, ours), (1 - column, there)):
        start = pl.multiple_of(x * QUARTER, QUARTER)
        for r, source in enumerate((here0, got0)):
            out[r * QUARTER : (r + 1) * QUARTER] = source[pl.ds(start, QUARTER)]
        out[HALF:] = marks.astype(BF16)
    for a, out in ((line, kept), (1.0 - line, sent)):
        for b in range(COARSE):
            total = 0.0
            for source in (here1, got1):
                into, mark = row_marks(source, 0), row_marks(source, 1)
                weight = (mark * a + (1.0 - mark) * (1.0 - a)) * (into if b else 1.0 - into)
                total = total + source[:HALF].astype(F32) * weight
            out[:, b * NB : (b + 1) * NB] = total.astype(out.dtype)


def below_sum_kernel(ours, theirs, kept, sent):
    line = (lax.axis_index("dev") // 4).astype(F32)
    marks = [v[HALF:].astype(F32) for v in (ours, theirs)]
    for a, out in ((line, kept), (1.0 - line, sent)):
        for b in range(COARSE):
            total = None
            for v, mark in zip((ours, theirs), marks):
                for r in range(2):
                    row_mark, into = mark[2 + r : 3 + r], mark[r : r + 1]
                    weight = (row_mark * a + (1.0 - row_mark) * (1.0 - a)) * (into if b else 1.0 - into)
                    value = v[r * QUARTER : (r + 1) * QUARTER].astype(F32) * weight
                    total = value if total is None else total + value
            out[:, b * NB : (b + 1) * NB] = total.astype(out.dtype)


def above_sum_kernel(ours, got, kept, sent):
    column = (lax.axis_index("dev") // 2) % 2
    for x, out in ((column, kept), (1 - column, sent)):
        at = pl.ds(pl.multiple_of(x * QUARTER, QUARTER), QUARTER)
        out[...] = (ours[at] + got[at].astype(F32)).astype(out.dtype)


def slab_kernel(left, b0, b1, b2, b3, b5, b6, b7, kept, sent0, sent1, held):
    core = lax.axis_index("dev") % 2
    for t, block in zip(TURNS, (b0, b1, b2, b3, b5, b6, b7)):
        value = dot(left[t], block[:NB])
        upper = block[NB:].astype(F32)[:1]
        for b, weight in enumerate((1.0 - upper, upper)):
            held[b] = value * weight if t == 0 else held[b] + value * weight
    for x in range(2):
        for b, sent in enumerate((sent0, sent1)):
            start = pl.multiple_of((2 * x + core) * QUARTER, QUARTER)
            kept[x * QUARTER : (x + 1) * QUARTER, b * NB : (b + 1) * NB] = held[b, pl.ds(start, QUARTER)]
            start = pl.multiple_of((2 * x + 1 - core) * QUARTER, QUARTER)
            sent[x * QUARTER : (x + 1) * QUARTER] = held[b, pl.ds(start, QUARTER)].astype(BF16)


def slab_sum_kernel(ours, got0, got1, b0, b1, kept, s2, s4, s6):
    place = lax.axis_index("dev")
    column, line = (place // 2) % 2, place // 4
    side = line.astype(F32)
    for a, outs in ((side, (kept, s2)), (1.0 - side, (s4, s6))):
        weights = []
        for block in (b0, b1):
            mark = block[NB:].astype(F32)[:1]
            weights.append(mark * a + (1.0 - mark) * (1.0 - a))
        for x, out in zip((column, 1 - column), outs):
            at = pl.ds(pl.multiple_of(x * QUARTER, QUARTER), QUARTER)
            for b, got in enumerate((got0, got1)):
                cut = slice(b * NB, (b + 1) * NB)
                out[:, cut] = (ours[at, cut] * weights[0] + got[at].astype(F32) * weights[1]).astype(out.dtype)


def last_kernel(below, got_below, kept, r2, r4, r6, above, got_above, out, held, sems):
    wide = COARSE * NB
    copies = []
    for side, parts in ((0, (below, got_below)), (2, (above, got_above)), (1, (kept, r2, r4, r6))):
        total = parts[0][...]
        for part in parts[1:]:
            total = total + part[...].astype(F32)
        held[side] = total
        copies.append(pltpu.make_async_copy(held.at[side], out.at[:, pl.ds(side * wide, wide)], sems.at[side]))
        copies[-1].start()
    for copy in copies:
        copy.wait()


def whole():
    return pl.BlockSpec(memory_space=pltpu.VMEM)


def scalars():
    return pl.BlockSpec(memory_space=pltpu.SMEM)


def call(kernel, name, outs, in_specs, scratch=(), out_specs=None):
    weight = WEIGHT.get(name)
    return pl.pallas_call(
        kernel,
        out_shape=tuple(jax.ShapeDtypeStruct(shape, kind) for shape, kind in outs),
        in_specs=in_specs,
        out_specs=out_specs or (whole(),) * len(outs),
        scratch_shapes=scratch,
        compiler_params=pltpu.CompilerParams(vmem_limit_bytes=16 * 2**20),
        cost_estimate=pl.CostEstimate(flops=weight, bytes_accessed=1000, transcendentals=0) if weight is not None else None,
        name=name,
    )


def after(value, *others):
    return lax.optimization_barrier((value, *others))[0]


def on_square(stiff_rows, stiff_iface, columns, live_count, aggregate, prolong):
    groups = lax.axis_size("grp")
    up = [(i, i + 1) for i in range(groups - 1)]
    down = [(j, i) for i, j in up]
    wide = COARSE * NB
    part, block, half = (QUARTER, wide), (MARKED, NB), (HALF + META, NB)

    def hop(array, turn):
        return lax.ppermute(array, "dev", [(i, i ^ turn) for i in range(8)])

    own = call(own_kernel, "own", ((block, BF16),), [whole()] * 2)(aggregate.reshape(1, 1), prolong)[0]
    b5 = hop(own, 5)
    b2 = hop(own, 2)
    below = lax.ppermute(own, "grp", up)
    above = lax.ppermute(own, "grp", down)
    b6 = hop(own, 6)
    columns, live_count = after((columns, live_count), b6)
    left, left_iface = call(
        left_kernel, "left", (((8, NB, NB), BF16), ((2, NB, NB), BF16)), [scalars()] * 2 + [whole()] * 3
    )(columns, live_count, stiff_rows, stiff_iface, own)
    here0, here1, away0, away1 = call(
        iface_kernel, "iface", ((half, BF16),) * 4, [whole()] * 4, [pltpu.VMEM((2, NB, NB), BF16)]
    )(left_iface, below, above, own)
    got0, got1 = hop(away0, 1), hop(away1, 1)
    ours, there, line_kept, line_sent = call(
        pack_kernel, "pack", ((half, BF16), (half, BF16), ((HALF, wide), F32), ((HALF, wide), BF16)), [whole()] * 4
    )(here0, here1, got0, after(got1, b5))
    theirs = hop(there, 2)
    below_kept, below_sent = call(below_sum_kernel, "below_sum", ((part, F32), (part, BF16)), [whole()] * 2)(
        ours, theirs
    )
    got_below = hop(below_sent, 4)
    b1 = hop(own, 1)
    b3 = hop(b2, 1)
    b7 = hop(after(b6, here0), 1)
    kept, sent0, sent1 = call(
        slab_kernel,
        "slab",
        (((HALF, wide), F32), ((HALF, NB), BF16), ((HALF, NB), BF16)),
        [whole()] * 8,
        [pltpu.VMEM((COARSE, NB, NB), F32)],
    )(left, own, b1, b2, b3, b5, b6, b7)
    sent = hop(sent0, 1), hop(sent1, 1)
    sum_kept, s2, s4, s6 = call(
        slab_sum_kernel, "slab_sum", ((part, F32), (part, BF16), (part, BF16), (part, BF16)), [whole()] * 5
    )(kept, sent[0], sent[1], own, b1)
    r2, r4, r6 = hop(s2, 2), hop(s4, 4), hop(s6, 6)
    got_line = hop(line_sent, 4)
    above_kept, above_sent = call(above_sum_kernel, "above_sum", ((part, F32), (part, BF16)), [whole()] * 2)(
        line_kept, got_line
    )
    got_above = hop(above_sent, 2)
    return call(
        last_kernel,
        "last",
        (((QUARTER, 3 * wide), F32),),
        [whole()] * 8,
        [pltpu.VMEM((3, QUARTER, wide), F32), pltpu.SemaphoreType.DMA((3,))],
        (pl.BlockSpec(memory_space=pltpu.HBM),),
    )(below_kept, got_below, sum_kept, r2, r4, r6, above_kept, got_above)[0]


def solution(mesh):
    in_specs = (
        P(("grp", "dev"), None, None, None),
        P(("grp", "dev"), None, None, None),
        P(("grp", "dev"), None),
        P(("grp", "dev")),
        P(("grp", "dev")),
        P(("grp", "dev"), None, None),
    )
    out_specs = P(("grp", "dev"), None)
    on_device = on_square if mesh.shape["dev"] == 8 else on_any_slab
    return jax.shard_map(
        on_device, mesh=mesh, in_specs=in_specs, out_specs=out_specs, check_vma=False
    )
```

time: 46.4 us -> 42.3 us (0.912)
  local copies, waits for them, and re-layouts: 2.55 us -> 0.97 us
  other arithmetic: 1.09 us -> 0 us
  starting transfers between devices: 22.3 us -> 21.5 us
  waiting for transfers between devices: 12.3 us -> 11.5 us
    ppermute x15 -> x17, waiting for transfers between devices: 12.3 us -> 9.71 us  [hop(): return lax.ppermute(array, 'dev', [(i, i ^ turn) for i in range(8)])]
    unnamed x6 -> x8, local copies, waits for them, and re-layouts: 2.55 us -> 0.97 us
    ppermute x1, waiting for transfers between devices: 0.01 us -> 1.18 us  [on_square(): below = lax.ppermute(own, 'grp', up)]
    select_n x1 -> x0, other arithmetic: 1.09 us -> none  [on_square(): own = jnp.where(block_row, longer, aggregate.astype(BF16)[:, None])]
    ppermute x15 -> x17, starting transfers between devices: 16.5 us -> 15.7 us  [hop(): return lax.ppermute(array, 'dev', [(i, i ^ turn) for i in range(8)])]
    ppermute x1, waiting for transfers between devices: 0.01 us -> 0.6 us  [on_square(): above = lax.ppermute(own, 'grp', down)]
    pallas_call x7 -> x8, Pallas kernels: 6.4 us -> 6.53 us  [the longest x1 2.57 us: on_square(): call(left_kernel, 'left', (((8, NB, NB), BF16), ((2, NB, NB), BF16)), [sc...]
  transfers between devices with their start and end apart: 17 -> 19, of which waited for: 7 -> 8; matrix products, arithmetic and copies ran while one was open for 0% -> 0% of each run, Pallas kernels for 12% -> 14%
where the time goes in v3:
time: 42.3 us; the launch traced here: 42.1 us
  starting transfers between devices  21.5 us (51%)
  waiting for transfers between devices  11.5 us (27%)
  Pallas kernels  6.73 us (16%)
  between operations  1.41 us (3%)
  local copies, waits for them, and re-layouts  0.97 us (2%)
    ppermute x17, starting transfers between devices, hop(): return lax.ppermute(array, 'dev', [(i, i ^ turn) for i in range(8)])  15.7 us
    ppermute x17, waiting for transfers between devices, hop(): return lax.ppermute(array, 'dev', [(i, i ^ turn) for i in range(8)])  9.71 us
    ppermute x1, starting transfers between devices, on_square(): below = lax.ppermute(own, 'grp', up)  4.57 us
    pallas_call x1, Pallas kernels, on_square(): call(left_kernel, 'left', (((8, NB, NB), BF16), ((2, NB, NB), BF16)), [sc...  2.57 us
    pallas_call x1, Pallas kernels, on_square(): call(slab_kernel, 'slab', (((HALF, wide), F32), ((HALF, NB), BF16), ((HAL...  1.68 us
    ppermute x1, starting transfers between devices, on_square(): above = lax.ppermute(own, 'grp', down)  1.28 us
    ppermute x1, waiting for transfers between devices, on_square(): below = lax.ppermute(own, 'grp', up)  1.18 us
    unnamed x8, local copies, waits for them, and re-layouts  0.97 us
  transfers between devices with their start and end apart: 19, of which 8 were waited for; matrix products, arithmetic and copies ran while one was open for 0% of the time, Pallas kernels for 14%

profile of v3, /device:TPU:0, one launch (start us, length us, event | category | flops | bytes accessed | tf_op | source)
XLA Modules:
  0.0 42.1 jit_solution(8085058058173233189)
XLA Ops:
  0.7 1.0 %copy-done.2 = bf16[1,384,384]{2,1,0:T(8,128)(2,1)S(1)} copy-done((bf16[1,384,384]{2,1,0:T(8,128)(2,1)S(1)}, bf16[1,384,384]{2,1,0:T(8,128)(2,1)}, u32[]{:S(2)}) %copy-start.2) | copy-done | bytes 294936
  1.7 3.9 %collective-permute-start = (bf16[400,384]{1,0:T(8,128)(2,1)S(1)}, bf16[400,384]{1,0:T(8,128)(2,1)S(1)}, u32[]{:S(2)}, u32[]{:S(2)}) collective-permute-start(bf16[400,384]{1,0:T(8,128)(2,1)S(1)} %own.1.b0), channel_id=1, source_target_pairs={{0,6},{1,7},{2,4},{3,5},{4,2},{5,3},{6,0},{7,1},{8,14},{9,15},{10,... | collective-permute-start | bytes 921608 | tf_op jit(solution)/shard_map/ppermute | solution.py:254
  5.6 1.3 %collective-permute-start.2 = (bf16[400,384]{1,0:T(8,128)(2,1)S(1)}, bf16[400,384]{1,0:T(8,128)(2,1)S(1)}, u32[]{:S(2)}, u32[]{:S(2)}) collective-permute-start(bf16[400,384]{1,0:T(8,128)(2,1)S(1)} %own.1.b0), channel_id=1, source_target_pairs={{8,0},{16,8},{24,16},{9,1},{17,9},{25,17},{10,2},{18,10},{26,18},{... | collective-permute-start | bytes 921608 | tf_op jit(solution)/shard_map/ppermute | solution.py:260
  6.9 4.6 %collective-permute-start.1 = (bf16[400,384]{1,0:T(8,128)(2,1)S(1)}, bf16[400,384]{1,0:T(8,128)(2,1)S(1)}, u32[]{:S(2)}, u32[]{:S(2)}) collective-permute-start(bf16[400,384]{1,0:T(8,128)(2,1)S(1)} %own.1.b0), channel_id=1, source_target_pairs={{0,8},{8,16},{16,24},{1,9},{9,17},{17,25},{2,10},{10,18},{18,26},{... | collective-permute-start | bytes 921608 | tf_op jit(solution)/shard_map/ppermute | solution.py:259
  11.5 0.6 %collective-permute-start.9 = (bf16[400,384]{1,0:T(8,128)(2,1)S(1)}, bf16[400,384]{1,0:T(8,128)(2,1)S(1)}, u32[]{:S(2)}, u32[]{:S(2)}) collective-permute-start(bf16[400,384]{1,0:T(8,128)(2,1)S(1)} %own.1.b0), channel_id=1, source_target_pairs={{0,2},{1,3},{2,0},{3,1},{4,6},{5,7},{6,4},{7,5},{8,10},{9,11},{10,... | collective-permute-start | bytes 921608 | tf_op jit(solution)/shard_map/ppermute | solution.py:254
  13.0 2.6 %left.1 = (bf16[8,384,384]{2,1,0:T(8,128)(2,1)S(1)}, bf16[2,384,384]{2,1,0:T(8,128)(2,1)S(1)}) custom-call(s32[1,6]{1,0:T(1,128)S(1)} %copy-done.3, s32[1]{0:T(128)S(6)} %copy.7.live, bf16[1,6,384,384]{3,2,1,0:T(8,128)(2,1)S(1)} %copy-done, bf16[1,2,384,384]{3,2,1,0:T(8,128)(2,1)S(1)} %copy-done.1, bf16[400,384]{1,0:T(8,128)(2,1)S(1)} %own.1.b0), custom_call_target="tpu_custom_call" | custom-call | flops 1000000000 | bytes 1000 | tf_op jit(solution)/shard_map/left/pallas_call | solution.py:263
  15.6 0.6 %collective-permute-done.2.above = bf16[400,384]{1,0:T(8,128)(2,1)S(1)} collective-permute-done((bf16[400,384]{1,0:T(8,128)(2,1)S(1)}, bf16[400,384]{1,0:T(8,128)(2,1)S(1)}, u32[]{:S(2)}, u32[]{:S(2)}) %collective-permute-start.2) | collective-permute-done | bytes 307232 | tf_op jit(solution)/shard_map/ppermute | solution.py:260
  16.2 1.2 %collective-permute-done.1.below = bf16[400,384]{1,0:T(8,128)(2,1)S(1)} collective-permute-done((bf16[400,384]{1,0:T(8,128)(2,1)S(1)}, bf16[400,384]{1,0:T(8,128)(2,1)S(1)}, u32[]{:S(2)}, u32[]{:S(2)}) %collective-permute-start.1) | collective-permute-done | bytes 307232 | tf_op jit(solution)/shard_map/ppermute | solution.py:259
  17.4 0.6 %iface.3 = (bf16[208,384]{1,0:T(8,128)(2,1)S(1)}, bf16[208,384]{1,0:T(8,128)(2,1)S(1)}, bf16[208,384]{1,0:T(8,128)(2,1)S(1)}, bf16[208,384]{1,0:T(8,128)(2,1)S(1)}) custom-call(bf16[2,384,384]{2,1,0:T(8,128)(2,1)S(1)} %get-tuple-element.32.left_iface, bf16[400,384]{1,0:T(8,128)(2,1)S(1)} %collective-permute-done.1.below, ...), custom_call_target="tpu_custom_call" | custom-call | flops 4000000000 | bytes 1000 | tf_op jit(solution)/shard_map/iface/pallas_call | solution.py:266
  18.1 0.5 %collective-permute-start.3 = (bf16[208,384]{1,0:T(8,128)(2,1)S(1)}, bf16[208,384]{1,0:T(8,128)(2,1)S(1)}, u32[]{:S(2)}, u32[]{:S(2)}) collective-permute-start(bf16[208,384]{1,0:T(8,128)(2,1)S(1)} %get-tuple-element.35), channel_id=1, source_target_pairs={{0,1},{1,0},{2,3},{3,2},{4,5},{5,4},{6,7},{7,6},{8,9},{9,8},{10,11... | collective-permute-start | bytes 479240 | tf_op jit(solution)/shard_map/ppermute | solution.py:254
  18.7 1.0 %collective-permute-done.9.b2 = bf16[400,384]{1,0:T(8,128)(2,1)S(1)} collective-permute-done((bf16[400,384]{1,0:T(8,128)(2,1)S(1)}, bf16[400,384]{1,0:T(8,128)(2,1)S(1)}, u32[]{:S(2)}, u32[]{:S(2)}) %collective-permute-start.9) | collective-permute-done | bytes 307232 | tf_op jit(solution)/shard_map/ppermute | solution.py:254
  19.7 0.8 %collective-permute-done.5.b5 = bf16[400,384]{1,0:T(8,128)(2,1)S(1)} collective-permute-done((bf16[400,384]{1,0:T(8,128)(2,1)S(1)}, bf16[400,384]{1,0:T(8,128)(2,1)S(1)}, u32[]{:S(2)}, u32[]{:S(2)}) %collective-permute-start.5) | collective-permute-done | bytes 307232 | tf_op jit(solution)/shard_map/ppermute | solution.py:254
  20.8 1.7 %collective-permute-start.6 = (bf16[208,384]{1,0:T(8,128)(2,1)S(1)}, bf16[208,384]{1,0:T(8,128)(2,1)S(1)}, u32[]{:S(2)}, u32[]{:S(2)}) collective-permute-start(bf16[208,384]{1,0:T(8,128)(2,1)S(1)} %get-tuple-element.39), channel_id=1, source_target_pairs={{0,2},{1,3},{2,0},{3,1},{4,6},{5,7},{6,4},{7,5},{8,10},{9,11},{10,... | collective-permute-start | bytes 479240 | tf_op jit(solution)/shard_map/ppermute | solution.py:254
  22.6 1.5 %collective-permute-start.17 = (bf16[192,768]{1,0:T(8,128)(2,1)S(1)}, bf16[192,768]{1,0:T(8,128)(2,1)S(1)}, u32[]{:S(2)}, u32[]{:S(2)}) collective-permute-start(bf16[192,768]{1,0:T(8,128)(2,1)S(1)} %get-tuple-element.52), channel_id=1, source_target_pairs={{0,4},{1,5},{2,6},{3,7},{4,0},{5,1},{6,2},{7,3},{8,12},{9,13},{10,... | collective-permute-start | bytes 884744 | tf_op jit(solution)/shard_map/ppermute | solution.py:254
  24.1 1.7 %slab.1 = (f32[192,768]{1,0:T(8,128)S(1)}, bf16[192,384]{1,0:T(8,128)(2,1)S(1)}, bf16[192,384]{1,0:T(8,128)(2,1)S(1)}) custom-call(bf16[8,384,384]{2,1,0:T(8,128)(2,1)S(1)} %get-tuple-element.42.left, bf16[400,384]{1,0:T(8,128)(2,1)S(1)} %own.1.b0, bf16[400,384]{1,0:T(8,128)(2,1)S(1)} %collective-permute-done.8.b1, ...), custom_call_target="tpu_custom_call" | custom-call | flops 4000000000 | bytes 1000 | tf_op jit(solution)/shard_map/slab/pallas_call | solution.py:281
  26.4 1.1 %collective-permute-done.6.theirs = bf16[208,384]{1,0:T(8,128)(2,1)S(1)} collective-permute-done((bf16[208,384]{1,0:T(8,128)(2,1)S(1)}, bf16[208,384]{1,0:T(8,128)(2,1)S(1)}, u32[]{:S(2)}, u32[]{:S(2)}) %collective-permute-start.6) | collective-permute-done | bytes 159776 | tf_op jit(solution)/shard_map/ppermute | solution.py:254
  27.7 1.4 %collective-permute-start.7 = (bf16[96,768]{1,0:T(8,128)(2,1)S(1)}, bf16[96,768]{1,0:T(8,128)(2,1)S(1)}, u32[]{:S(2)}, u32[]{:S(2)}) collective-permute-start(bf16[96,768]{1,0:T(8,128)(2,1)S(1)} %get-tuple-element.41), channel_id=1, source_target_pairs={{0,4},{1,5},{2,6},{3,7},{4,0},{5,1},{6,2},{7,3},{8,12},{9,13},{10,... | collective-permute-start | bytes 442376 | tf_op jit(solution)/shard_map/ppermute | solution.py:254
  29.3 1.8 %collective-permute-start.14 = (bf16[96,768]{1,0:T(8,128)(2,1)S(1)}, bf16[96,768]{1,0:T(8,128)(2,1)S(1)}, u32[]{:S(2)}, u32[]{:S(2)}) collective-permute-start(bf16[96,768]{1,0:T(8,128)(2,1)S(1)} %get-tuple-element.48), channel_id=1, source_target_pairs={{0,2},{1,3},{2,0},{3,1},{4,6},{5,7},{6,4},{7,5},{8,10},{9,11},{10,... | collective-permute-start | bytes 442376 | tf_op jit(solution)/shard_map/ppermute | solution.py:254
  31.1 0.6 %collective-permute-start.15 = (bf16[96,768]{1,0:T(8,128)(2,1)S(1)}, bf16[96,768]{1,0:T(8,128)(2,1)S(1)}, u32[]{:S(2)}, u32[]{:S(2)}) collective-permute-start(bf16[96,768]{1,0:T(8,128)(2,1)S(1)} %get-tuple-element.49), channel_id=1, source_target_pairs={{0,4},{1,5},{2,6},{3,7},{4,0},{5,1},{6,2},{7,3},{8,12},{9,13},{10,... | collective-permute-start | bytes 442376 | tf_op jit(solution)/shard_map/ppermute | solution.py:254
  31.7 1.1 %collective-permute-start.16 = (bf16[96,768]{1,0:T(8,128)(2,1)S(1)}, bf16[96,768]{1,0:T(8,128)(2,1)S(1)}, u32[]{:S(2)}, u32[]{:S(2)}) collective-permute-start(bf16[96,768]{1,0:T(8,128)(2,1)S(1)} %get-tuple-element.50), channel_id=1, source_target_pairs={{0,6},{1,7},{2,4},{3,5},{4,2},{5,3},{6,0},{7,1},{8,14},{9,15},{10,... | collective-permute-start | bytes 442376 | tf_op jit(solution)/shard_map/ppermute | solution.py:254
  32.9 1.8 %collective-permute-start.18 = (bf16[96,768]{1,0:T(8,128)(2,1)S(1)}, bf16[96,768]{1,0:T(8,128)(2,1)S(1)}, u32[]{:S(2)}, u32[]{:S(2)}) collective-permute-start(bf16[96,768]{1,0:T(8,128)(2,1)S(1)} %get-tuple-element.54), channel_id=1, source_target_pairs={{0,2},{1,3},{2,0},{3,1},{4,6},{5,7},{6,4},{7,5},{8,10},{9,11},{10,... | collective-permute-start | bytes 442376 | tf_op jit(solution)/shard_map/ppermute | solution.py:254
  34.7 3.3 %collective-permute-done.7.got_below = bf16[96,768]{1,0:T(8,128)(2,1)S(1)} collective-permute-done((bf16[96,768]{1,0:T(8,128)(2,1)S(1)}, bf16[96,768]{1,0:T(8,128)(2,1)S(1)}, u32[]{:S(2)}, u32[]{:S(2)}) %collective-permute-start.7) | collective-permute-done | bytes 147488 | tf_op jit(solution)/shard_map/ppermute | solution.py:254
  38.0 3.2 %collective-permute-done.15.r4 = bf16[96,768]{1,0:T(8,128)(2,1)S(1)} collective-permute-done((bf16[96,768]{1,0:T(8,128)(2,1)S(1)}, bf16[96,768]{1,0:T(8,128)(2,1)S(1)}, u32[]{:S(2)}, u32[]{:S(2)}) %collective-permute-start.15) | collective-permute-done | bytes 147488 | tf_op jit(solution)/shard_map/ppermute | solution.py:254
  41.2 1.0 %last.1 = f32[96,2304]{1,0:T(8,128)} custom-call(f32[96,768]{1,0:T(8,128)S(1)} %get-tuple-element.40.below, bf16[96,768]{1,0:T(8,128)(2,1)S(1)} %collective-permute-done.7.got_below, f32[96,768]{1,0:T(8,128)S(1)} %get-tuple-element.47.kept, bf16[96,768]{1,0:T(8,128)(2,1)S(1)} %collective-permute-done.14.r2, bf16[96,768]{1,0:T(8,128)(2,1)S(1)} %collective-permute-done.15.r4, ...), custom_call_target="tpu_custom_call" | custom-call | flops 4000000000 | bytes 1000 | tf_op jit(solution)/shard_map/last/pallas_call | solution.py:298
  (31 shorter events, 2.0 us)
Async XLA Ops:
  0.7 1.0 %copy-start.2 = (bf16[1,384,384]{2,1,0:T(8,128)(2,1)S(1)}, bf16[1,384,384]{2,1,0:T(8,128)(2,1)}, u32[]{:S(2)}) copy-start(bf16[1,384,384]{2,1,0:T(8,128)(2,1)} %prolong.1) | copy-start | bytes 884740
  1.6 11.4 %copy-start = (bf16[1,6,384,384]{3,2,1,0:T(8,128)(2,1)S(1)}, bf16[1,6,384,384]{3,2,1,0:T(8,128)(2,1)}, u32[]{:S(2)}) copy-start(bf16[1,6,384,384]{3,2,1,0:T(8,128)(2,1)} %rows.1) | copy-start | bytes 5308420
  1.6 11.4 %copy-start.1 = (bf16[1,2,384,384]{3,2,1,0:T(8,128)(2,1)S(1)}, bf16[1,2,384,384]{3,2,1,0:T(8,128)(2,1)}, u32[]{:S(2)}) copy-start(bf16[1,2,384,384]{3,2,1,0:T(8,128)(2,1)} %iface.2) | copy-start | bytes 1769476
  1.6 11.4 %copy-start.3 = (s32[1,6]{1,0:T(1,128)S(1)}, s32[1,6]{1,0:T(1,128)}, u32[]{:S(2)}) copy-start(s32[1,6]{1,0:T(1,128)} %columns) | copy-start | bytes 76
  1.7 11.3 %collective-permute-start = (bf16[400,384]{1,0:T(8,128)(2,1)S(1)}, bf16[400,384]{1,0:T(8,128)(2,1)S(1)}, u32[]{:S(2)}, u32[]{:S(2)}) collective-permute-start(bf16[400,384]{1,0:T(8,128)(2,1)S(1)} %own.1.b0), channel_id=1, source_target_pairs={{0,6},{1,7},{2,4},{3,5},{4,2},{5,3},{6,0},{7,1},{8,14},{9,15},{10,... | collective-permute-start | bytes 921608 | tf_op jit(solution)/shard_map/ppermute | solution.py:254
  5.6 10.6 %collective-permute-start.2 = (bf16[400,384]{1,0:T(8,128)(2,1)S(1)}, bf16[400,384]{1,0:T(8,128)(2,1)S(1)}, u32[]{:S(2)}, u32[]{:S(2)}) collective-permute-start(bf16[400,384]{1,0:T(8,128)(2,1)S(1)} %own.1.b0), channel_id=1, source_target_pairs={{8,0},{16,8},{24,16},{9,1},{17,9},{25,17},{10,2},{18,10},{26,18},{... | collective-permute-start | bytes 921608 | tf_op jit(solution)/shard_map/ppermute | solution.py:260
  6.9 10.5 %collective-permute-start.1 = (bf16[400,384]{1,0:T(8,128)(2,1)S(1)}, bf16[400,384]{1,0:T(8,128)(2,1)S(1)}, u32[]{:S(2)}, u32[]{:S(2)}) collective-permute-start(bf16[400,384]{1,0:T(8,128)(2,1)S(1)} %own.1.b0), channel_id=1, source_target_pairs={{0,8},{8,16},{16,24},{1,9},{9,17},{17,25},{2,10},{10,18},{18,26},{... | collective-permute-start | bytes 921608 | tf_op jit(solution)/shard_map/ppermute | solution.py:259
  11.5 8.2 %collective-permute-start.9 = (bf16[400,384]{1,0:T(8,128)(2,1)S(1)}, bf16[400,384]{1,0:T(8,128)(2,1)S(1)}, u32[]{:S(2)}, u32[]{:S(2)}) collective-permute-start(bf16[400,384]{1,0:T(8,128)(2,1)S(1)} %own.1.b0), channel_id=1, source_target_pairs={{0,2},{1,3},{2,0},{3,1},{4,6},{5,7},{6,4},{7,5},{8,10},{9,11},{10,... | collective-permute-start | bytes 921608 | tf_op jit(solution)/shard_map/ppermute | solution.py:254
  12.1 8.5 %collective-permute-start.5 = (bf16[400,384]{1,0:T(8,128)(2,1)S(1)}, bf16[400,384]{1,0:T(8,128)(2,1)S(1)}, u32[]{:S(2)}, u32[]{:S(2)}) collective-permute-start(bf16[400,384]{1,0:T(8,128)(2,1)S(1)} %own.1.b0), channel_id=1, source_target_pairs={{0,5},{1,4},{2,7},{3,6},{4,1},{5,0},{6,3},{7,2},{8,13},{9,12},{10,... | collective-permute-start | bytes 921608 | tf_op jit(solution)/shard_map/ppermute | solution.py:254
  18.0 2.5 %collective-permute-start.4 = (bf16[208,384]{1,0:T(8,128)(2,1)S(1)}, bf16[208,384]{1,0:T(8,128)(2,1)S(1)}, u32[]{:S(2)}, u32[]{:S(2)}) collective-permute-start(bf16[208,384]{1,0:T(8,128)(2,1)S(1)} %get-tuple-element.36), channel_id=1, source_target_pairs={{0,1},{1,0},{2,3},{3,2},{4,5},{5,4},{6,7},{7,6},{8,9},{9,8},{10,11... | collective-permute-start | bytes 479240 | tf_op jit(solution)/shard_map/ppermute | solution.py:254
  18.1 2.4 %collective-permute-start.3 = (bf16[208,384]{1,0:T(8,128)(2,1)S(1)}, bf16[208,384]{1,0:T(8,128)(2,1)S(1)}, u32[]{:S(2)}, u32[]{:S(2)}) collective-permute-start(bf16[208,384]{1,0:T(8,128)(2,1)S(1)} %get-tuple-element.35), channel_id=1, source_target_pairs={{0,1},{1,0},{2,3},{3,2},{4,5},{5,4},{6,7},{7,6},{8,9},{9,8},{10,11... | collective-permute-start | bytes 479240 | tf_op jit(solution)/shard_map/ppermute | solution.py:254
  18.6 5.4 %collective-permute-start.8 = (bf16[400,384]{1,0:T(8,128)(2,1)S(1)}, bf16[400,384]{1,0:T(8,128)(2,1)S(1)}, u32[]{:S(2)}, u32[]{:S(2)}) collective-permute-start(bf16[400,384]{1,0:T(8,128)(2,1)S(1)} %own.1.b0), channel_id=1, source_target_pairs={{0,1},{1,0},{2,3},{3,2},{4,5},{5,4},{6,7},{7,6},{8,9},{9,8},{10,11... | collective-permute-start | bytes 921608 | tf_op jit(solution)/shard_map/ppermute | solution.py:254
  19.7 4.4 %collective-permute-start.11 = (bf16[400,384]{1,0:T(8,128)(2,1)S(1)}, bf16[400,384]{1,0:T(8,128)(2,1)S(1)}, u32[]{:S(2)}, u32[]{:S(2)}) collective-permute-start(bf16[400,384]{1,0:T(8,128)(2,1)S(1)} %collective-permute-done.b6), channel_id=1, source_target_pairs={{0,1},{1,0},{2,3},{3,2},{4,5},{5,4},{6,7},{7,6},{8,9},{9,8},{10,11... | collective-permute-start | bytes 921608 | tf_op jit(solution)/shard_map/ppermute | solution.py:254
  20.5 3.5 %collective-permute-start.10 = (bf16[400,384]{1,0:T(8,128)(2,1)S(1)}, bf16[400,384]{1,0:T(8,128)(2,1)S(1)}, u32[]{:S(2)}, u32[]{:S(2)}) collective-permute-start(bf16[400,384]{1,0:T(8,128)(2,1)S(1)} %collective-permute-done.9.b2), channel_id=1, source_target_pairs={{0,1},{1,0},{2,3},{3,2},{4,5},{5,4},{6,7},{7,6},{8,9},{9,8},{10,11... | collective-permute-start | bytes 921608 | tf_op jit(solution)/shard_map/ppermute | solution.py:254
  20.8 6.6 %collective-permute-start.6 = (bf16[208,384]{1,0:T(8,128)(2,1)S(1)}, bf16[208,384]{1,0:T(8,128)(2,1)S(1)}, u32[]{:S(2)}, u32[]{:S(2)}) collective-permute-start(bf16[208,384]{1,0:T(8,128)(2,1)S(1)} %get-tuple-element.39), channel_id=1, source_target_pairs={{0,2},{1,3},{2,0},{3,1},{4,6},{5,7},{6,4},{7,5},{8,10},{9,11},{10,... | collective-permute-start | bytes 479240 | tf_op jit(solution)/shard_map/ppermute | solution.py:254
  22.6 10.3 %collective-permute-start.17 = (bf16[192,768]{1,0:T(8,128)(2,1)S(1)}, bf16[192,768]{1,0:T(8,128)(2,1)S(1)}, u32[]{:S(2)}, u32[]{:S(2)}) collective-permute-start(bf16[192,768]{1,0:T(8,128)(2,1)S(1)} %get-tuple-element.52), channel_id=1, source_target_pairs={{0,4},{1,5},{2,6},{3,7},{4,0},{5,1},{6,2},{7,3},{8,12},{9,13},{10,... | collective-permute-start | bytes 884744 | tf_op jit(solution)/shard_map/ppermute | solution.py:254
  25.8 3.3 %collective-permute-start.12 = (bf16[192,384]{1,0:T(8,128)(2,1)S(1)}, bf16[192,384]{1,0:T(8,128)(2,1)S(1)}, u32[]{:S(2)}, u32[]{:S(2)}) collective-permute-start(bf16[192,384]{1,0:T(8,128)(2,1)S(1)} %get-tuple-element.45), channel_id=1, source_target_pairs={{0,1},{1,0},{2,3},{3,2},{4,5},{5,4},{6,7},{7,6},{8,9},{9,8},{10,11... | collective-permute-start | bytes 442376 | tf_op jit(solution)/shard_map/ppermute | solution.py:254
  25.9 3.2 %collective-permute-start.13 = (bf16[192,384]{1,0:T(8,128)(2,1)S(1)}, bf16[192,384]{1,0:T(8,128)(2,1)S(1)}, u32[]{:S(2)}, u32[]{:S(2)}) collective-permute-start(bf16[192,384]{1,0:T(8,128)(2,1)S(1)} %get-tuple-element.46), channel_id=1, source_target_pairs={{0,1},{1,0},{2,3},{3,2},{4,5},{5,4},{6,7},{7,6},{8,9},{9,8},{10,11... | collective-permute-start | bytes 442376 | tf_op jit(solution)/shard_map/ppermute | solution.py:254
  27.7 10.3 %collective-permute-start.7 = (bf16[96,768]{1,0:T(8,128)(2,1)S(1)}, bf16[96,768]{1,0:T(8,128)(2,1)S(1)}, u32[]{:S(2)}, u32[]{:S(2)}) collective-permute-start(bf16[96,768]{1,0:T(8,128)(2,1)S(1)} %get-tuple-element.41), channel_id=1, source_target_pairs={{0,4},{1,5},{2,6},{3,7},{4,0},{5,1},{6,2},{7,3},{8,12},{9,13},{10,... | collective-permute-start | bytes 442376 | tf_op jit(solution)/shard_map/ppermute | solution.py:254
  29.3 8.7 %collective-permute-start.14 = (bf16[96,768]{1,0:T(8,128)(2,1)S(1)}, bf16[96,768]{1,0:T(8,128)(2,1)S(1)}, u32[]{:S(2)}, u32[]{:S(2)}) collective-permute-start(bf16[96,768]{1,0:T(8,128)(2,1)S(1)} %get-tuple-element.48), channel_id=1, source_target_pairs={{0,2},{1,3},{2,0},{3,1},{4,6},{5,7},{6,4},{7,5},{8,10},{9,11},{10,... | collective-permute-start | bytes 442376 | tf_op jit(solution)/shard_map/ppermute | solution.py:254
  31.1 10.1 %collective-permute-start.15 = (bf16[96,768]{1,0:T(8,128)(2,1)S(1)}, bf16[96,768]{1,0:T(8,128)(2,1)S(1)}, u32[]{:S(2)}, u32[]{:S(2)}) collective-permute-start(bf16[96,768]{1,0:T(8,128)(2,1)S(1)} %get-tuple-element.49), channel_id=1, source_target_pairs={{0,4},{1,5},{2,6},{3,7},{4,0},{5,1},{6,2},{7,3},{8,12},{9,13},{10,... | collective-permute-start | bytes 442376 | tf_op jit(solution)/shard_map/ppermute | solution.py:254
  31.7 9.5 %collective-permute-start.16 = (bf16[96,768]{1,0:T(8,128)(2,1)S(1)}, bf16[96,768]{1,0:T(8,128)(2,1)S(1)}, u32[]{:S(2)}, u32[]{:S(2)}) collective-permute-start(bf16[96,768]{1,0:T(8,128)(2,1)S(1)} %get-tuple-element.50), channel_id=1, source_target_pairs={{0,6},{1,7},{2,4},{3,5},{4,2},{5,3},{6,0},{7,1},{8,14},{9,15},{10,... | collective-permute-start | bytes 442376 | tf_op jit(solution)/shard_map/ppermute | solution.py:254
  32.9 8.3 %collective-permute-start.18 = (bf16[96,768]{1,0:T(8,128)(2,1)S(1)}, bf16[96,768]{1,0:T(8,128)(2,1)S(1)}, u32[]{:S(2)}, u32[]{:S(2)}) collective-permute-start(bf16[96,768]{1,0:T(8,128)(2,1)S(1)} %get-tuple-element.54), channel_id=1, source_target_pairs={{0,2},{1,3},{2,0},{3,1},{4,6},{5,7},{6,4},{7,5},{8,10},{9,11},{10,... | collective-permute-start | bytes 442376 | tf_op jit(solution)/shard_map/ppermute | solution.py:254

commit v4 on v3

--- a/solution.py
+++ b/solution.py
@@ -92,9 +92,12 @@
     return jnp.dot(a, b, preferred_element_type=F32)
 
 
-def own_kernel(aggregate, prolong, own):
-    own[:NB] = prolong[0]
-    own[NB:] = jnp.broadcast_to(aggregate[...], (META, NB)).astype(F32).astype(BF16)
+def own_kernel(aggregate, prolong, own, longer):
+    mark = jnp.broadcast_to(aggregate[...], (META, NB)).astype(F32).astype(BF16)
+    for out in (own, longer):
+        out[:NB] = prolong[0]
+        for start in range(NB, out.shape[0], META):
+            out[start : start + META] = mark
 
 
 def left_kernel(columns, live, rows, iface, own, left, left_iface):
@@ -115,7 +118,7 @@
     row = lax.broadcasted_iota(jnp.int32, (META, NB), 0)
     for s, (block, here, away) in enumerate(((below, here0, away0), (above, here1, away1))):
         held[s] = dot(left_iface[s], block[:NB]).astype(BF16)
-        marks = jnp.where(row == 0, block[NB:].astype(F32), own[NB:].astype(F32)).astype(BF16)
+        marks = jnp.where(row == 0, block[NB:MARKED].astype(F32), own[NB:].astype(F32)).astype(BF16)
         for c, out in ((core, here), (1 - core, away)):
             for x in range(2):
                 start = pl.multiple_of((2 * x + c) * QUARTER, QUARTER)
@@ -253,10 +256,12 @@
     def hop(array, turn):
         return lax.ppermute(array, "dev", [(i, i ^ turn) for i in range(8)])
 
-    own = call(own_kernel, "own", ((block, BF16),), [whole()] * 2)(aggregate.reshape(1, 1), prolong)[0]
+    own, longer = call(own_kernel, "own", ((block, BF16), ((MARKED + META, NB), BF16)), [whole()] * 2)(
+        aggregate.reshape(1, 1), prolong
+    )
     b5 = hop(own, 5)
     b2 = hop(own, 2)
-    below = lax.ppermute(own, "grp", up)
+    below = lax.ppermute(longer, "grp", up)
     above = lax.ppermute(own, "grp", down)
     b6 = hop(own, 6)
     columns, live_count = after((columns, live_count), b6)

time: 42.3 us -> 42.2 us (level)
  starting transfers between devices: 21.5 us -> 17.9 us
  waiting for transfers between devices: 11.5 us -> 14.4 us
  Pallas kernels: 6.73 us -> 7.36 us
    ppermute x17, starting transfers between devices: 15.7 us -> 13.2 us  [hop(): return lax.ppermute(array, 'dev', [(i, i ^ turn) for i in range(8)])]
    ppermute x1, waiting for transfers between devices: 0.6 us -> 2.79 us  [on_square(): above = lax.ppermute(own, 'grp', down)]
    ppermute x17, waiting for transfers between devices: 9.71 us -> 11.6 us  [hop(): return lax.ppermute(array, 'dev', [(i, i ^ turn) for i in range(8)])]
    ppermute x1, waiting for transfers between devices: 1.18 us -> 0.01 us  [on_square(): below = lax.ppermute(longer, 'grp', up)]
    ppermute x1, starting transfers between devices: 4.57 us -> 3.49 us  [on_square(): below = lax.ppermute(longer, 'grp', up)]
    pallas_call x1, Pallas kernels: 2.57 us -> 3.23 us  [on_square(): call(left_kernel, 'left', (((8, NB, NB), BF16), ((2, NB, NB), BF16)), [sc...]
  transfers between devices with their start and end apart: 19 -> 19, of which waited for: 8 -> 7; matrix products, arithmetic and copies ran while one was open for 0% -> 0% of each run, Pallas kernels for 14% -> 15%
where the time goes in v4:
time: 42.2 us; the launch traced here: 42 us
  starting transfers between devices  17.9 us (42%)
  waiting for transfers between devices  14.4 us (34%)
  Pallas kernels  7.36 us (17%)
  between operations  1.41 us (3%)
  local copies, waits for them, and re-layouts  0.97 us (2%)
    ppermute x17, starting transfers between devices, hop(): return lax.ppermute(array, 'dev', [(i, i ^ turn) for i in range(8)])  13.2 us
    ppermute x17, waiting for transfers between devices, hop(): return lax.ppermute(array, 'dev', [(i, i ^ turn) for i in range(8)])  11.6 us
    ppermute x1, starting transfers between devices, on_square(): below = lax.ppermute(longer, 'grp', up)  3.49 us
    pallas_call x1, Pallas kernels, on_square(): call(left_kernel, 'left', (((8, NB, NB), BF16), ((2, NB, NB), BF16)), [sc...  3.23 us
    ppermute x1, waiting for transfers between devices, on_square(): above = lax.ppermute(own, 'grp', down)  2.79 us
    pallas_call x1, Pallas kernels, on_square(): call(slab_kernel, 'slab', (((HALF, wide), F32), ((HALF, NB), BF16), ((HAL...  1.68 us
    ppermute x1, starting transfers between devices, on_square(): above = lax.ppermute(own, 'grp', down)  1.29 us
    unnamed x8, local copies, waits for them, and re-layouts  0.97 us
  transfers between devices with their start and end apart: 19, of which 7 were waited for; matrix products, arithmetic and copies ran while one was open for 0% of the time, Pallas kernels for 15%

profile of v4, /device:TPU:0, one launch (start us, length us, event | category | flops | bytes accessed | tf_op | source)
XLA Modules:
  0.0 42.0 jit_solution(8676720883724677888)
XLA Ops:
  0.7 1.0 %copy-done.2 = bf16[1,384,384]{2,1,0:T(8,128)(2,1)S(1)} copy-done((bf16[1,384,384]{2,1,0:T(8,128)(2,1)S(1)}, bf16[1,384,384]{2,1,0:T(8,128)(2,1)}, u32[]{:S(2)}) %copy-start.2) | copy-done | bytes 294936
  1.7 3.9 %collective-permute-start = (bf16[400,384]{1,0:T(8,128)(2,1)S(1)}, bf16[400,384]{1,0:T(8,128)(2,1)S(1)}, u32[]{:S(2)}, u32[]{:S(2)}) collective-permute-start(bf16[400,384]{1,0:T(8,128)(2,1)S(1)} %get-tuple-element.32.own.b0), channel_id=1, source_target_pairs={{0,6},{1,7},{2,4},{3,5},{4,2},{5,3},{6,0},{7,1},{8,14},{9,15},{10,... | collective-permute-start | bytes 921608 | tf_op jit(solution)/shard_map/ppermute | solution.py:257
  5.6 3.5 %collective-permute-start.1 = (bf16[416,384]{1,0:T(8,128)(2,1)S(1)}, bf16[416,384]{1,0:T(8,128)(2,1)S(1)}, u32[]{:S(2)}, u32[]{:S(2)}) collective-permute-start(bf16[416,384]{1,0:T(8,128)(2,1)S(1)} %get-tuple-element.36), channel_id=1, source_target_pairs={{0,8},{8,16},{16,24},{1,9},{9,17},{17,25},{2,10},{10,18},{18,26},{... | collective-permute-start | bytes 958472 | tf_op jit(solution)/shard_map/ppermute | solution.py:264
  9.1 1.3 %collective-permute-start.2 = (bf16[400,384]{1,0:T(8,128)(2,1)S(1)}, bf16[400,384]{1,0:T(8,128)(2,1)S(1)}, u32[]{:S(2)}, u32[]{:S(2)}) collective-permute-start(bf16[400,384]{1,0:T(8,128)(2,1)S(1)} %get-tuple-element.32.own.b0), channel_id=1, source_target_pairs={{8,0},{16,8},{24,16},{9,1},{17,9},{25,17},{10,2},{18,10},{26,18},{... | collective-permute-start | bytes 921608 | tf_op jit(solution)/shard_map/ppermute | solution.py:265
  10.4 0.6 %collective-permute-start.9 = (bf16[400,384]{1,0:T(8,128)(2,1)S(1)}, bf16[400,384]{1,0:T(8,128)(2,1)S(1)}, u32[]{:S(2)}, u32[]{:S(2)}) collective-permute-start(bf16[400,384]{1,0:T(8,128)(2,1)S(1)} %get-tuple-element.32.own.b0), channel_id=1, source_target_pairs={{0,2},{1,3},{2,0},{3,1},{4,6},{5,7},{6,4},{7,5},{8,10},{9,11},{10,... | collective-permute-start | bytes 921608 | tf_op jit(solution)/shard_map/ppermute | solution.py:257
  11.7 1.8 %collective-permute-done.b6 = bf16[400,384]{1,0:T(8,128)(2,1)S(1)} collective-permute-done((bf16[400,384]{1,0:T(8,128)(2,1)S(1)}, bf16[400,384]{1,0:T(8,128)(2,1)S(1)}, u32[]{:S(2)}, u32[]{:S(2)}) %collective-permute-start) | collective-permute-done | bytes 307232 | tf_op jit(solution)/shard_map/ppermute | solution.py:257
  13.5 3.2 %left.1 = (bf16[8,384,384]{2,1,0:T(8,128)(2,1)S(1)}, bf16[2,384,384]{2,1,0:T(8,128)(2,1)S(1)}) custom-call(s32[1,6]{1,0:T(1,128)S(1)} %copy-done.3, s32[1]{0:T(128)S(6)} %copy.7.live, bf16[1,6,384,384]{3,2,1,0:T(8,128)(2,1)S(1)} %copy-done, bf16[1,2,384,384]{3,2,1,0:T(8,128)(2,1)S(1)} %copy-done.1, bf16[400,384]{1,0:T(8,128)(2,1)S(1)} %get-tuple-element.32.own.b0), custom_call_target="tpu_custom_call" | custom-call | flops 1000000000 | bytes 1000 | tf_op jit(solution)/shard_map/left/pallas_call | solution.py:268
  16.7 2.8 %collective-permute-done.2.above = bf16[400,384]{1,0:T(8,128)(2,1)S(1)} collective-permute-done((bf16[400,384]{1,0:T(8,128)(2,1)S(1)}, bf16[400,384]{1,0:T(8,128)(2,1)S(1)}, u32[]{:S(2)}, u32[]{:S(2)}) %collective-permute-start.2) | collective-permute-done | bytes 307232 | tf_op jit(solution)/shard_map/ppermute | solution.py:265
  19.5 0.6 %iface.3 = (bf16[208,384]{1,0:T(8,128)(2,1)S(1)}, bf16[208,384]{1,0:T(8,128)(2,1)S(1)}, bf16[208,384]{1,0:T(8,128)(2,1)S(1)}, bf16[208,384]{1,0:T(8,128)(2,1)S(1)}) custom-call(bf16[2,384,384]{2,1,0:T(8,128)(2,1)S(1)} %get-tuple-element.35.left_iface, bf16[416,384]{1,0:T(8,128)(2,1)S(1)} %collective-permute-done.1.below, ...), custom_call_target="tpu_custom_call" | custom-call | flops 4000000000 | bytes 1000 | tf_op jit(solution)/shard_map/iface/pallas_call | solution.py:271
  20.2 0.5 %collective-permute-start.3 = (bf16[208,384]{1,0:T(8,128)(2,1)S(1)}, bf16[208,384]{1,0:T(8,128)(2,1)S(1)}, u32[]{:S(2)}, u32[]{:S(2)}) collective-permute-start(bf16[208,384]{1,0:T(8,128)(2,1)S(1)} %get-tuple-element.39), channel_id=1, source_target_pairs={{0,1},{1,0},{2,3},{3,2},{4,5},{5,4},{6,7},{7,6},{8,9},{9,8},{10,11... | collective-permute-start | bytes 479240 | tf_op jit(solution)/shard_map/ppermute | solution.py:257
  20.8 0.4 %collective-permute-start.10 = (bf16[400,384]{1,0:T(8,128)(2,1)S(1)}, bf16[400,384]{1,0:T(8,128)(2,1)S(1)}, u32[]{:S(2)}, u32[]{:S(2)}) collective-permute-start(bf16[400,384]{1,0:T(8,128)(2,1)S(1)} %collective-permute-done.9.b2), channel_id=1, source_target_pairs={{0,1},{1,0},{2,3},{3,2},{4,5},{5,4},{6,7},{7,6},{8,9},{9,8},{10,11... | collective-permute-start | bytes 921608 | tf_op jit(solution)/shard_map/ppermute | solution.py:257
  22.1 0.6 %collective-permute-start.6 = (bf16[208,384]{1,0:T(8,128)(2,1)S(1)}, bf16[208,384]{1,0:T(8,128)(2,1)S(1)}, u32[]{:S(2)}, u32[]{:S(2)}) collective-permute-start(bf16[208,384]{1,0:T(8,128)(2,1)S(1)} %get-tuple-element.43), channel_id=1, source_target_pairs={{0,2},{1,3},{2,0},{3,1},{4,6},{5,7},{6,4},{7,5},{8,10},{9,11},{10,... | collective-permute-start | bytes 479240 | tf_op jit(solution)/shard_map/ppermute | solution.py:257
  22.7 1.0 %collective-permute-start.17 = (bf16[192,768]{1,0:T(8,128)(2,1)S(1)}, bf16[192,768]{1,0:T(8,128)(2,1)S(1)}, u32[]{:S(2)}, u32[]{:S(2)}) collective-permute-start(bf16[192,768]{1,0:T(8,128)(2,1)S(1)} %get-tuple-element.56), channel_id=1, source_target_pairs={{0,4},{1,5},{2,6},{3,7},{4,0},{5,1},{6,2},{7,3},{8,12},{9,13},{10,... | collective-permute-start | bytes 884744 | tf_op jit(solution)/shard_map/ppermute | solution.py:257
  23.7 1.7 %slab.1 = (f32[192,768]{1,0:T(8,128)S(1)}, bf16[192,384]{1,0:T(8,128)(2,1)S(1)}, bf16[192,384]{1,0:T(8,128)(2,1)S(1)}) custom-call(bf16[8,384,384]{2,1,0:T(8,128)(2,1)S(1)} %get-tuple-element.46.left, bf16[400,384]{1,0:T(8,128)(2,1)S(1)} %get-tuple-element.32.own.b0, bf16[400,384]{1,0:T(8,128)(2,1)S(1)} %collective-permute-done.8.b1, ...), custom_call_target="tpu_custom_call" | custom-call | flops 4000000000 | bytes 1000 | tf_op jit(solution)/shard_map/slab/pallas_call | solution.py:286
  25.5 0.5 %collective-permute-start.13 = (bf16[192,384]{1,0:T(8,128)(2,1)S(1)}, bf16[192,384]{1,0:T(8,128)(2,1)S(1)}, u32[]{:S(2)}, u32[]{:S(2)}) collective-permute-start(bf16[192,384]{1,0:T(8,128)(2,1)S(1)} %get-tuple-element.50), channel_id=1, source_target_pairs={{0,1},{1,0},{2,3},{3,2},{4,5},{5,4},{6,7},{7,6},{8,9},{9,8},{10,11... | collective-permute-start | bytes 442376 | tf_op jit(solution)/shard_map/ppermute | solution.py:257
  25.9 2.5 %collective-permute-done.6.theirs = bf16[208,384]{1,0:T(8,128)(2,1)S(1)} collective-permute-done((bf16[208,384]{1,0:T(8,128)(2,1)S(1)}, bf16[208,384]{1,0:T(8,128)(2,1)S(1)}, u32[]{:S(2)}, u32[]{:S(2)}) %collective-permute-start.6) | collective-permute-done | bytes 159776 | tf_op jit(solution)/shard_map/ppermute | solution.py:257
  28.7 0.6 %collective-permute-start.7 = (bf16[96,768]{1,0:T(8,128)(2,1)S(1)}, bf16[96,768]{1,0:T(8,128)(2,1)S(1)}, u32[]{:S(2)}, u32[]{:S(2)}) collective-permute-start(bf16[96,768]{1,0:T(8,128)(2,1)S(1)} %get-tuple-element.45), channel_id=1, source_target_pairs={{0,4},{1,5},{2,6},{3,7},{4,0},{5,1},{6,2},{7,3},{8,12},{9,13},{10,... | collective-permute-start | bytes 442376 | tf_op jit(solution)/shard_map/ppermute | solution.py:257
  29.5 1.2 %collective-permute-start.14 = (bf16[96,768]{1,0:T(8,128)(2,1)S(1)}, bf16[96,768]{1,0:T(8,128)(2,1)S(1)}, u32[]{:S(2)}, u32[]{:S(2)}) collective-permute-start(bf16[96,768]{1,0:T(8,128)(2,1)S(1)} %get-tuple-element.52), channel_id=1, source_target_pairs={{0,2},{1,3},{2,0},{3,1},{4,6},{5,7},{6,4},{7,5},{8,10},{9,11},{10,... | collective-permute-start | bytes 442376 | tf_op jit(solution)/shard_map/ppermute | solution.py:257
  30.7 0.9 %collective-permute-start.15 = (bf16[96,768]{1,0:T(8,128)(2,1)S(1)}, bf16[96,768]{1,0:T(8,128)(2,1)S(1)}, u32[]{:S(2)}, u32[]{:S(2)}) collective-permute-start(bf16[96,768]{1,0:T(8,128)(2,1)S(1)} %get-tuple-element.53), channel_id=1, source_target_pairs={{0,4},{1,5},{2,6},{3,7},{4,0},{5,1},{6,2},{7,3},{8,12},{9,13},{10,... | collective-permute-start | bytes 442376 | tf_op jit(solution)/shard_map/ppermute | solution.py:257
  31.6 1.4 %collective-permute-start.16 = (bf16[96,768]{1,0:T(8,128)(2,1)S(1)}, bf16[96,768]{1,0:T(8,128)(2,1)S(1)}, u32[]{:S(2)}, u32[]{:S(2)}) collective-permute-start(bf16[96,768]{1,0:T(8,128)(2,1)S(1)} %get-tuple-element.54), channel_id=1, source_target_pairs={{0,6},{1,7},{2,4},{3,5},{4,2},{5,3},{6,0},{7,1},{8,14},{9,15},{10,... | collective-permute-start | bytes 442376 | tf_op jit(solution)/shard_map/ppermute | solution.py:257
  33.1 1.2 %collective-permute-start.18 = (bf16[96,768]{1,0:T(8,128)(2,1)S(1)}, bf16[96,768]{1,0:T(8,128)(2,1)S(1)}, u32[]{:S(2)}, u32[]{:S(2)}) collective-permute-start(bf16[96,768]{1,0:T(8,128)(2,1)S(1)} %get-tuple-element.58), channel_id=1, source_target_pairs={{0,2},{1,3},{2,0},{3,1},{4,6},{5,7},{6,4},{7,5},{8,10},{9,11},{10,... | collective-permute-start | bytes 442376 | tf_op jit(solution)/shard_map/ppermute | solution.py:257
  34.3 2.9 %collective-permute-done.7.got_below = bf16[96,768]{1,0:T(8,128)(2,1)S(1)} collective-permute-done((bf16[96,768]{1,0:T(8,128)(2,1)S(1)}, bf16[96,768]{1,0:T(8,128)(2,1)S(1)}, u32[]{:S(2)}, u32[]{:S(2)}) %collective-permute-start.7) | collective-permute-done | bytes 147488 | tf_op jit(solution)/shard_map/ppermute | solution.py:257
  37.1 3.9 %collective-permute-done.15.r4 = bf16[96,768]{1,0:T(8,128)(2,1)S(1)} collective-permute-done((bf16[96,768]{1,0:T(8,128)(2,1)S(1)}, bf16[96,768]{1,0:T(8,128)(2,1)S(1)}, u32[]{:S(2)}, u32[]{:S(2)}) %collective-permute-start.15) | collective-permute-done | bytes 147488 | tf_op jit(solution)/shard_map/ppermute | solution.py:257
  41.1 1.0 %last.1 = f32[96,2304]{1,0:T(8,128)} custom-call(f32[96,768]{1,0:T(8,128)S(1)} %get-tuple-element.44.below, bf16[96,768]{1,0:T(8,128)(2,1)S(1)} %collective-permute-done.7.got_below, f32[96,768]{1,0:T(8,128)S(1)} %get-tuple-element.51.kept, bf16[96,768]{1,0:T(8,128)(2,1)S(1)} %collective-permute-done.14.r2, bf16[96,768]{1,0:T(8,128)(2,1)S(1)} %collective-permute-done.15.r4, ...), custom_call_target="tpu_custom_call" | custom-call | flops 4000000000 | bytes 1000 | tf_op jit(solution)/shard_map/last/pallas_call | solution.py:303
  (31 shorter events, 1.7 us)
Async XLA Ops:
  0.7 1.0 %copy-start.2 = (bf16[1,384,384]{2,1,0:T(8,128)(2,1)S(1)}, bf16[1,384,384]{2,1,0:T(8,128)(2,1)}, u32[]{:S(2)}) copy-start(bf16[1,384,384]{2,1,0:T(8,128)(2,1)} %prolong.1) | copy-start | bytes 884740
  1.6 11.8 %copy-start = (bf16[1,6,384,384]{3,2,1,0:T(8,128)(2,1)S(1)}, bf16[1,6,384,384]{3,2,1,0:T(8,128)(2,1)}, u32[]{:S(2)}) copy-start(bf16[1,6,384,384]{3,2,1,0:T(8,128)(2,1)} %rows.1) | copy-start | bytes 5308420
  1.6 11.8 %copy-start.1 = (bf16[1,2,384,384]{3,2,1,0:T(8,128)(2,1)S(1)}, bf16[1,2,384,384]{3,2,1,0:T(8,128)(2,1)}, u32[]{:S(2)}) copy-start(bf16[1,2,384,384]{3,2,1,0:T(8,128)(2,1)} %iface.2) | copy-start | bytes 1769476
  1.6 11.8 %copy-start.3 = (s32[1,6]{1,0:T(1,128)S(1)}, s32[1,6]{1,0:T(1,128)}, u32[]{:S(2)}) copy-start(s32[1,6]{1,0:T(1,128)} %columns) | copy-start | bytes 76
  1.7 11.7 %collective-permute-start = (bf16[400,384]{1,0:T(8,128)(2,1)S(1)}, bf16[400,384]{1,0:T(8,128)(2,1)S(1)}, u32[]{:S(2)}, u32[]{:S(2)}) collective-permute-start(bf16[400,384]{1,0:T(8,128)(2,1)S(1)} %get-tuple-element.32.own.b0), channel_id=1, source_target_pairs={{0,6},{1,7},{2,4},{3,5},{4,2},{5,3},{6,0},{7,1},{8,14},{9,15},{10,... | collective-permute-start | bytes 921608 | tf_op jit(solution)/shard_map/ppermute | solution.py:257
  5.6 13.8 %collective-permute-start.1 = (bf16[416,384]{1,0:T(8,128)(2,1)S(1)}, bf16[416,384]{1,0:T(8,128)(2,1)S(1)}, u32[]{:S(2)}, u32[]{:S(2)}) collective-permute-start(bf16[416,384]{1,0:T(8,128)(2,1)S(1)} %get-tuple-element.36), channel_id=1, source_target_pairs={{0,8},{8,16},{16,24},{1,9},{9,17},{17,25},{2,10},{10,18},{18,26},{... | collective-permute-start | bytes 958472 | tf_op jit(solution)/shard_map/ppermute | solution.py:264
  9.1 10.3 %collective-permute-start.2 = (bf16[400,384]{1,0:T(8,128)(2,1)S(1)}, bf16[400,384]{1,0:T(8,128)(2,1)S(1)}, u32[]{:S(2)}, u32[]{:S(2)}) collective-permute-start(bf16[400,384]{1,0:T(8,128)(2,1)S(1)} %get-tuple-element.32.own.b0), channel_id=1, source_target_pairs={{8,0},{16,8},{24,16},{9,1},{17,9},{25,17},{10,2},{18,10},{26,18},{... | collective-permute-start | bytes 921608 | tf_op jit(solution)/shard_map/ppermute | solution.py:265
  10.4 10.4 %collective-permute-start.9 = (bf16[400,384]{1,0:T(8,128)(2,1)S(1)}, bf16[400,384]{1,0:T(8,128)(2,1)S(1)}, u32[]{:S(2)}, u32[]{:S(2)}) collective-permute-start(bf16[400,384]{1,0:T(8,128)(2,1)S(1)} %get-tuple-element.32.own.b0), channel_id=1, source_target_pairs={{0,2},{1,3},{2,0},{3,1},{4,6},{5,7},{6,4},{7,5},{8,10},{9,11},{10,... | collective-permute-start | bytes 921608 | tf_op jit(solution)/shard_map/ppermute | solution.py:257
  11.0 10.2 %collective-permute-start.5 = (bf16[400,384]{1,0:T(8,128)(2,1)S(1)}, bf16[400,384]{1,0:T(8,128)(2,1)S(1)}, u32[]{:S(2)}, u32[]{:S(2)}) collective-permute-start(bf16[400,384]{1,0:T(8,128)(2,1)S(1)} %get-tuple-element.32.own.b0), channel_id=1, source_target_pairs={{0,5},{1,4},{2,7},{3,6},{4,1},{5,0},{6,3},{7,2},{8,13},{9,12},{10,... | collective-permute-start | bytes 921608 | tf_op jit(solution)/shard_map/ppermute | solution.py:257
  20.1 1.5 %collective-permute-start.4 = (bf16[208,384]{1,0:T(8,128)(2,1)S(1)}, bf16[208,384]{1,0:T(8,128)(2,1)S(1)}, u32[]{:S(2)}, u32[]{:S(2)}) collective-permute-start(bf16[208,384]{1,0:T(8,128)(2,1)S(1)} %get-tuple-element.40), channel_id=1, source_target_pairs={{0,1},{1,0},{2,3},{3,2},{4,5},{5,4},{6,7},{7,6},{8,9},{9,8},{10,11... | collective-permute-start | bytes 479240 | tf_op jit(solution)/shard_map/ppermute | solution.py:257
  20.2 1.6 %collective-permute-start.3 = (bf16[208,384]{1,0:T(8,128)(2,1)S(1)}, bf16[208,384]{1,0:T(8,128)(2,1)S(1)}, u32[]{:S(2)}, u32[]{:S(2)}) collective-permute-start(bf16[208,384]{1,0:T(8,128)(2,1)S(1)} %get-tuple-element.39), channel_id=1, source_target_pairs={{0,1},{1,0},{2,3},{3,2},{4,5},{5,4},{6,7},{7,6},{8,9},{9,8},{10,11... | collective-permute-start | bytes 479240 | tf_op jit(solution)/shard_map/ppermute | solution.py:257
  20.7 3.0 %collective-permute-start.8 = (bf16[400,384]{1,0:T(8,128)(2,1)S(1)}, bf16[400,384]{1,0:T(8,128)(2,1)S(1)}, u32[]{:S(2)}, u32[]{:S(2)}) collective-permute-start(bf16[400,384]{1,0:T(8,128)(2,1)S(1)} %get-tuple-element.32.own.b0), channel_id=1, source_target_pairs={{0,1},{1,0},{2,3},{3,2},{4,5},{5,4},{6,7},{7,6},{8,9},{9,8},{10,11... | collective-permute-start | bytes 921608 | tf_op jit(solution)/shard_map/ppermute | solution.py:257
  20.8 2.9 %collective-permute-start.10 = (bf16[400,384]{1,0:T(8,128)(2,1)S(1)}, bf16[400,384]{1,0:T(8,128)(2,1)S(1)}, u32[]{:S(2)}, u32[]{:S(2)}) collective-permute-start(bf16[400,384]{1,0:T(8,128)(2,1)S(1)} %collective-permute-done.9.b2), channel_id=1, source_target_pairs={{0,1},{1,0},{2,3},{3,2},{4,5},{5,4},{6,7},{7,6},{8,9},{9,8},{10,11... | collective-permute-start | bytes 921608 | tf_op jit(solution)/shard_map/ppermute | solution.py:257
  21.2 2.5 %collective-permute-start.11 = (bf16[400,384]{1,0:T(8,128)(2,1)S(1)}, bf16[400,384]{1,0:T(8,128)(2,1)S(1)}, u32[]{:S(2)}, u32[]{:S(2)}) collective-permute-start(bf16[400,384]{1,0:T(8,128)(2,1)S(1)} %collective-permute-done.b6), channel_id=1, source_target_pairs={{0,1},{1,0},{2,3},{3,2},{4,5},{5,4},{6,7},{7,6},{8,9},{9,8},{10,11... | collective-permute-start | bytes 921608 | tf_op jit(solution)/shard_map/ppermute | solution.py:257
  22.1 6.4 %collective-permute-start.6 = (bf16[208,384]{1,0:T(8,128)(2,1)S(1)}, bf16[208,384]{1,0:T(8,128)(2,1)S(1)}, u32[]{:S(2)}, u32[]{:S(2)}) collective-permute-start(bf16[208,384]{1,0:T(8,128)(2,1)S(1)} %get-tuple-element.43), channel_id=1, source_target_pairs={{0,2},{1,3},{2,0},{3,1},{4,6},{5,7},{6,4},{7,5},{8,10},{9,11},{10,... | collective-permute-start | bytes 479240 | tf_op jit(solution)/shard_map/ppermute | solution.py:257
  22.7 10.4 %collective-permute-start.17 = (bf16[192,768]{1,0:T(8,128)(2,1)S(1)}, bf16[192,768]{1,0:T(8,128)(2,1)S(1)}, u32[]{:S(2)}, u32[]{:S(2)}) collective-permute-start(bf16[192,768]{1,0:T(8,128)(2,1)S(1)} %get-tuple-element.56), channel_id=1, source_target_pairs={{0,4},{1,5},{2,6},{3,7},{4,0},{5,1},{6,2},{7,3},{8,12},{9,13},{10,... | collective-permute-start | bytes 884744 | tf_op jit(solution)/shard_map/ppermute | solution.py:257
  25.4 3.9 %collective-permute-start.12 = (bf16[192,384]{1,0:T(8,128)(2,1)S(1)}, bf16[192,384]{1,0:T(8,128)(2,1)S(1)}, u32[]{:S(2)}, u32[]{:S(2)}) collective-permute-start(bf16[192,384]{1,0:T(8,128)(2,1)S(1)} %get-tuple-element.49), channel_id=1, source_target_pairs={{0,1},{1,0},{2,3},{3,2},{4,5},{5,4},{6,7},{7,6},{8,9},{9,8},{10,11... | collective-permute-start | bytes 442376 | tf_op jit(solution)/shard_map/ppermute | solution.py:257
  25.5 3.8 %collective-permute-start.13 = (bf16[192,384]{1,0:T(8,128)(2,1)S(1)}, bf16[192,384]{1,0:T(8,128)(2,1)S(1)}, u32[]{:S(2)}, u32[]{:S(2)}) collective-permute-start(bf16[192,384]{1,0:T(8,128)(2,1)S(1)} %get-tuple-element.50), channel_id=1, source_target_pairs={{0,1},{1,0},{2,3},{3,2},{4,5},{5,4},{6,7},{7,6},{8,9},{9,8},{10,11... | collective-permute-start | bytes 442376 | tf_op jit(solution)/shard_map/ppermute | solution.py:257
  28.7 8.4 %collective-permute-start.7 = (bf16[96,768]{1,0:T(8,128)(2,1)S(1)}, bf16[96,768]{1,0:T(8,128)(2,1)S(1)}, u32[]{:S(2)}, u32[]{:S(2)}) collective-permute-start(bf16[96,768]{1,0:T(8,128)(2,1)S(1)} %get-tuple-element.45), channel_id=1, source_target_pairs={{0,4},{1,5},{2,6},{3,7},{4,0},{5,1},{6,2},{7,3},{8,12},{9,13},{10,... | collective-permute-start | bytes 442376 | tf_op jit(solution)/shard_map/ppermute | solution.py:257
  29.5 7.6 %collective-permute-start.14 = (bf16[96,768]{1,0:T(8,128)(2,1)S(1)}, bf16[96,768]{1,0:T(8,128)(2,1)S(1)}, u32[]{:S(2)}, u32[]{:S(2)}) collective-permute-start(bf16[96,768]{1,0:T(8,128)(2,1)S(1)} %get-tuple-element.52), channel_id=1, source_target_pairs={{0,2},{1,3},{2,0},{3,1},{4,6},{5,7},{6,4},{7,5},{8,10},{9,11},{10,... | collective-permute-start | bytes 442376 | tf_op jit(solution)/shard_map/ppermute | solution.py:257
  30.7 10.4 %collective-permute-start.15 = (bf16[96,768]{1,0:T(8,128)(2,1)S(1)}, bf16[96,768]{1,0:T(8,128)(2,1)S(1)}, u32[]{:S(2)}, u32[]{:S(2)}) collective-permute-start(bf16[96,768]{1,0:T(8,128)(2,1)S(1)} %get-tuple-element.53), channel_id=1, source_target_pairs={{0,4},{1,5},{2,6},{3,7},{4,0},{5,1},{6,2},{7,3},{8,12},{9,13},{10,... | collective-permute-start | bytes 442376 | tf_op jit(solution)/shard_map/ppermute | solution.py:257
  31.6 9.5 %collective-permute-start.16 = (bf16[96,768]{1,0:T(8,128)(2,1)S(1)}, bf16[96,768]{1,0:T(8,128)(2,1)S(1)}, u32[]{:S(2)}, u32[]{:S(2)}) collective-permute-start(bf16[96,768]{1,0:T(8,128)(2,1)S(1)} %get-tuple-element.54), channel_id=1, source_target_pairs={{0,6},{1,7},{2,4},{3,5},{4,2},{5,3},{6,0},{7,1},{8,14},{9,15},{10,... | collective-permute-start | bytes 442376 | tf_op jit(solution)/shard_map/ppermute | solution.py:257
  33.1 8.0 %collective-permute-start.18 = (bf16[96,768]{1,0:T(8,128)(2,1)S(1)}, bf16[96,768]{1,0:T(8,128)(2,1)S(1)}, u32[]{:S(2)}, u32[]{:S(2)}) collective-permute-start(bf16[96,768]{1,0:T(8,128)(2,1)S(1)} %get-tuple-element.58), channel_id=1, source_target_pairs={{0,2},{1,3},{2,0},{3,1},{4,6},{5,7},{6,4},{7,5},{8,10},{9,11},{10,... | collective-permute-start | bytes 442376 | tf_op jit(solution)/shard_map/ppermute | solution.py:257
